TPU v7x, 32 devices: a whole 2x2x4 slice. The times are simulated.
32 devices in a mesh: head: 8 (over z, y), blk: 4 (over x, core).
Axes of the slice: x: 2, y: 2, z: 4, core: 2. Of those that a mesh axis runs over, the one named last changes fastest.
Arguments:
- inputs: bfloat16 [2, 4, 1024, 1024], P(None, 'blk', 'head'), may hold values from -6 to 6
- segments: int32 [2, 4, 1024], replicated, may hold values from 0 to 8, as said below
- bucket_table: int32 [257], replicated, may hold values from 0 to 31, as said below
- norm_gain: bfloat16 [1024], P(('head', 'blk')), may hold values from 0.25 to 1.75
- w_query: bfloat16 [1024, 1024], P(('head', 'blk')), may hold values from -0.09375 to 0.09375
- w_key: bfloat16 [1024, 1024], P(('head', 'blk')), may hold values from -0.09375 to 0.09375
- w_value: bfloat16 [1024, 1024], P(('head', 'blk')), may hold values from -0.1875 to 0.1875
- w_out: bfloat16 [1024, 1024], P(('head', 'blk')), may hold values from -0.375 to 0.375
- rel_bias: bfloat16 [512], P(('head', 'blk')), may hold values from -4 to 4
- ff_gain: bfloat16 [1024], P(('head', 'blk')), may hold values from 0.25 to 1.75
- w_in: bfloat16 [1024, 4096], P(('head', 'blk')), may hold values from -0.1875 to 0.1875
- w_down: bfloat16 [4096, 1024], P(('head', 'blk')), may hold values from -0.09375 to 0.09375
- cotangent: bfloat16 [2, 4, 1024, 1024], P(None, 'blk', 'head'), may hold values from -6 to 6
Outputs:
- layer_out: bfloat16 [2, 4, 1024, 1024], P(None, 'blk', 'head')
- input_grad: bfloat16 [2, 4, 1024, 1024], P(None, 'blk', 'head')
- grad_norm_gain: float32 [1024], P(('head', 'blk'))
- grad_query: float32 [1024, 1024], P(('head', 'blk'))
- grad_key: float32 [1024, 1024], P(('head', 'blk'))
- grad_value: float32 [1024, 1024], P(('head', 'blk'))
- grad_out: float32 [1024, 1024], P(('head', 'blk'))
- grad_rel: float32 [512], P(('head', 'blk'))
- grad_ff_gain: float32 [1024], P(('head', 'blk'))
- grad_in: float32 [1024, 4096], P(('head', 'blk'))
- grad_down: float32 [4096, 1024], P(('head', 'blk'))
Inputs may be any that keep to these rules, and one draw needn't show every extreme that they name: `segments`: document numbers start at 0 in each sequence and never fall along it. In one sequence drawn from the seed the whole sequence is one document; in every other one each aligned run of min(512, 4096) positions holds exactly one document start, lying at least an eighth of the run away from the run's ends. `bucket_table`: A relabelling drawn from the seed of the bidirectional T5 buckets (32 buckets; exact distances below a quarter of them on each side, logarithmic up to 128) for offsets minus 128 to 128; entry 128 is offset 0.
All inputs are finite; a program needn't handle non-finite values.
Results may differ from a plain program's by a relative error of at most 0.02.
Values may be sent and summed in bfloat16 or wider, within the bound.
No kernel may reach another device: no remote copies, remote signals or barrier semaphores. Data moves between devices by JAX's collectives and lax.ppermute only.
A program may use at most 256 MiB of HBM per device.

v0:
```python
import functools

import jax
import jax.numpy as jnp
import numpy as np
from jax import lax
from jax.experimental import pallas as pl
from jax.experimental.pallas import tpu as pltpu
from jax.sharding import PartitionSpec as P

HEADS = 16
HD = 64
BUCKETS = 32
MAXREL = 128
EPS = 1e-06
FLOOR = -1e30


def from_behind(block, axis, distance):
    devices = range(lax.axis_size(axis))
    route = [((i - distance) % len(devices), i) for i in devices]
    return lax.ppermute(block, axis, route)


def rms_scale(token_rows, gain_vector):
    return (
        token_rows
        * lax.rsqrt(jnp.mean(token_rows * token_rows, axis=-1, keepdims=True) + EPS)
        * gain_vector
    )


def smooth(values):
    return jax.nn.gelu(values, approximate=True)


def band_layout(span_len):
    tile_side = min(128, span_len)
    reach = MAXREL // tile_side + 2
    return (tile_side, span_len // tile_side, reach)


def band_tables(bucket_table, rel_here, span_len):
    tile_side, _, reach = band_layout(span_len)
    kinds = 2 * reach + 1
    gaps = lax.iota(jnp.int32, kinds) - reach
    rows_in = lax.iota(jnp.int32, tile_side)
    offsets = gaps[:, None, None] * tile_side + rows_in[None, None, :] - rows_in[None, :, None]
    lookup = jnp.clip(offsets, -MAXREL, MAXREL) + MAXREL
    bucket = jnp.take(bucket_table, lookup.reshape(-1), axis=0)
    onehot = (bucket[:, None] == lax.iota(jnp.int32, BUCKETS)[None, :]).astype(jnp.float32)
    band_bias = jnp.dot(rel_here, onehot.T, precision=lax.Precision.HIGHEST)
    return (band_bias.reshape(rel_here.shape[0], kinds, tile_side, tile_side), onehot)


def band_index(block_gap, span_len):
    _, tiles, reach = band_layout(span_len)
    row_tile = lax.iota(jnp.int32, tiles)[:, None, None, None]
    col_tile = lax.iota(jnp.int32, tiles)[None, None, :, None]
    return jnp.clip(block_gap * tiles + col_tile - row_tile, -reach, reach) + reach


def bias_tile(band_bias, block_gap, span_len):
    heads_count, kinds, tile_side, _ = band_bias.shape
    tiles = span_len // tile_side
    which = band_index(block_gap, span_len)
    result = jnp.zeros((heads_count, tiles, tile_side, tiles, tile_side), jnp.float32)
    for kind in range(kinds):
        result = jnp.where(which[None] == kind, band_bias[:, kind][:, None, :, None, :], result)
    return result.reshape(heads_count, span_len, span_len)


def band_sums(tile_sum, block_gap, span_len):
    tile_side, tiles, reach = band_layout(span_len)
    heads_count = tile_sum.shape[0]
    split_sum = tile_sum.reshape(heads_count, tiles, tile_side, tiles, tile_side)
    which = band_index(block_gap, span_len)
    parts = []
    for kind in range(2 * reach + 1):
        parts.append(jnp.sum(jnp.where(which[None] == kind, split_sum, 0.0), axis=(1, 3)))
    return jnp.stack(parts, axis=1).reshape(heads_count, -1)


def pass_grads(key_grad, value_grad):
    return (
        from_behind(key_grad.astype(jnp.bfloat16), "blk", 1).astype(key_grad.dtype),
        from_behind(value_grad.astype(jnp.bfloat16), "blk", 1).astype(value_grad.dtype),
    )


def ring_body(
    inputs,
    segments,
    bucket_table,
    norm_gain,
    w_query,
    w_key,
    w_value,
    w_out,
    rel_bias,
    ff_gain,
    w_in,
    w_down,
    cotangent,
):
    seq_count, _, part_len, width = inputs.shape
    cycle_size = lax.axis_size("blk")
    head_groups = lax.axis_size("head")
    heads_here = HEADS // head_groups
    span_len = part_len * head_groups
    cycle_place = lax.axis_index("blk")
    head_place = lax.axis_index("head")
    gathered = (
        lax.all_gather(norm_gain, ("head", "blk"), axis=0, tiled=True),
        lax.all_gather(w_query, ("head", "blk"), axis=0, tiled=True),
        lax.all_gather(w_key, ("head", "blk"), axis=0, tiled=True),
        lax.all_gather(w_value, ("head", "blk"), axis=0, tiled=True),
        lax.all_gather(w_out, ("head", "blk"), axis=0, tiled=True),
        lax.all_gather(rel_bias, ("head", "blk"), axis=0, tiled=True),
        lax.all_gather(ff_gain, ("head", "blk"), axis=0, tiled=True),
        lax.all_gather(w_in, ("head", "blk"), axis=0, tiled=True),
        lax.all_gather(w_down, ("head", "blk"), axis=0, tiled=True),
    )
    gain_one, query_w, key_w, value_w, out_w, rel_flat, gain_two, in_w, down_w = gathered
    token_rows = inputs.reshape(-1, width).astype(jnp.float32)
    normed, norm_one_back = jax.vjp(rms_scale, token_rows, gain_one.astype(jnp.float32))
    first_in = normed.astype(jnp.bfloat16)

    def project(weight):
        made_rows = jnp.dot(first_in, weight, preferred_element_type=jnp.float32)
        return made_rows.astype(jnp.bfloat16).reshape(seq_count, part_len, -1)

    queries, keys_home, values_home = (
        lax.all_to_all(project(query_w), "head", split_axis=2, concat_axis=1, tiled=True),
        lax.all_to_all(project(key_w), "head", split_axis=2, concat_axis=1, tiled=True),
        lax.all_to_all(project(value_w), "head", split_axis=2, concat_axis=1, tiled=True),
    )
    head_shape = (seq_count, span_len, heads_here, HD)
    queries = queries.reshape(head_shape)
    keys_home = keys_home.reshape(head_shape)
    values_home = values_home.reshape(head_shape)
    rel_table = rel_flat.astype(jnp.float32).reshape(HEADS, BUCKETS)
    rel_here = lax.dynamic_slice_in_dim(rel_table, head_place * heads_here, heads_here, 0)
    band_bias, band_onehot = band_tables(bucket_table, rel_here, span_len)

    def tile_scores(query_rows, key_rows, query_block, key_block):
        query_ids = lax.dynamic_index_in_dim(segments, query_block, 1, keepdims=False)
        key_ids = lax.dynamic_index_in_dim(segments, key_block, 1, keepdims=False)
        plain_scores = (
            jnp.einsum("sihd,sjhd->shij", query_rows, key_rows, preferred_element_type=jnp.float32)
            + bias_tile(band_bias, key_block - query_block, span_len)[None]
        )
        same_doc = query_ids[:, None, :, None] == key_ids[:, None, None, :]
        return jnp.where(same_doc, plain_scores, FLOOR)

    first_scores = tile_scores(queries, keys_home, cycle_place, cycle_place)
    row_max = jnp.max(first_scores, axis=-1)
    first_weights = jnp.exp(first_scores - row_max[..., None])
    row_total = jnp.sum(first_weights, axis=-1)
    summed = jnp.einsum(
        "shij,sjhd->sihd",
        first_weights.astype(jnp.bfloat16),
        values_home,
        preferred_element_type=jnp.float32,
    )

    def forward_turn(cycle_turn, state_now):
        old_max, old_total, old_summed, key_rows, value_rows = state_now
        key_rows, value_rows = from_behind((key_rows, value_rows), "blk", 1)
        source = (cycle_place - cycle_turn) % cycle_size
        scores = tile_scores(queries, key_rows, cycle_place, source)
        new_max = jnp.maximum(old_max, jnp.max(scores, axis=-1))
        shrink = jnp.exp(old_max - new_max)
        weights_now = jnp.exp(scores - new_max[..., None])
        new_total = old_total * shrink + jnp.sum(weights_now, axis=-1)
        new_summed = old_summed * jnp.transpose(shrink, (0, 2, 1))[..., None] + jnp.einsum(
            "shij,sjhd->sihd",
            weights_now.astype(jnp.bfloat16),
            value_rows,
            preferred_element_type=jnp.float32,
        )
        return (new_max, new_total, new_summed, key_rows, value_rows)

    row_max, row_total, summed, _, _ = lax.fori_loop(
        1, cycle_size, forward_turn, (row_max, row_total, summed, keys_home, values_home)
    )
    log_total = row_max + jnp.log(row_total)
    attended = summed / jnp.transpose(row_total, (0, 2, 1))[..., None]
    attended_low = attended.astype(jnp.bfloat16).reshape(seq_count, span_len, heads_here * HD)
    attn_rows = lax.all_to_all(
        attended_low, "head", split_axis=1, concat_axis=2, tiled=True
    ).reshape(-1, HEADS * HD)
    hidden_one = token_rows + jnp.dot(attn_rows, out_w, preferred_element_type=jnp.float32)
    normed_two, norm_two_back = jax.vjp(rms_scale, hidden_one, gain_two.astype(jnp.float32))
    second_in = normed_two.astype(jnp.bfloat16)
    upward = jnp.dot(second_in, in_w, preferred_element_type=jnp.float32)
    activated, smooth_back = jax.vjp(smooth, upward)
    activated_low = activated.astype(jnp.bfloat16)
    layer_rows = hidden_one + jnp.dot(activated_low, down_w, preferred_element_type=jnp.float32)
    layer_out = layer_rows.astype(jnp.bfloat16).reshape(inputs.shape)
    back_query, back_key, back_value, back_out, back_in, back_down = (
        query_w,
        key_w,
        value_w,
        out_w,
        in_w,
        down_w,
    )
    incoming_low = cotangent.reshape(-1, width)
    incoming = incoming_low.astype(jnp.float32)
    grad_down = jnp.dot(activated_low.T, incoming_low, preferred_element_type=jnp.float32)
    (up_grad,) = smooth_back(jnp.dot(incoming_low, back_down.T, preferred_element_type=jnp.float32))
    up_low = up_grad.astype(jnp.bfloat16)
    grad_in = jnp.dot(second_in.T, up_low, preferred_element_type=jnp.float32)
    hidden_part, grad_gain_two = norm_two_back(
        jnp.dot(up_low, back_in.T, preferred_element_type=jnp.float32)
    )
    hidden_grad = incoming + hidden_part
    branch_low = hidden_grad.astype(jnp.bfloat16)
    grad_out = jnp.dot(attn_rows.T, branch_low, preferred_element_type=jnp.float32)
    attn_grad_low = jnp.dot(branch_low, back_out.T, preferred_element_type=jnp.float32).astype(
        jnp.bfloat16
    )
    grad_heads = lax.all_to_all(
        attn_grad_low.reshape(seq_count, part_len, HEADS * HD),
        "head",
        split_axis=2,
        concat_axis=1,
        tiled=True,
    ).reshape(head_shape)
    row_delta = jnp.transpose(
        jnp.sum(grad_heads.astype(jnp.float32) * attended, axis=-1), (0, 2, 1)
    )

    def tile_grads(
        query_rows, grad_rows, log_rows, delta_rows, key_rows, value_rows, query_block, key_block
    ):
        scores = tile_scores(query_rows, key_rows, query_block, key_block)
        probs = jnp.exp(scores - log_rows[..., None])
        value_part = jnp.einsum(
            "shij,sihd->sjhd",
            probs.astype(jnp.bfloat16),
            grad_rows,
            preferred_element_type=jnp.float32,
        )
        prob_grad = jnp.einsum(
            "sihd,sjhd->shij", grad_rows, value_rows, preferred_element_type=jnp.float32
        )
        score_low = (probs * (prob_grad - delta_rows[..., None])).astype(jnp.bfloat16)
        query_part = jnp.einsum(
            "shij,sjhd->sihd", score_low, key_rows, preferred_element_type=jnp.float32
        )
        key_part = jnp.einsum(
            "shij,sihd->sjhd", score_low, query_rows, preferred_element_type=jnp.float32
        )
        tile_sum = jnp.sum(score_low.astype(jnp.float32), axis=0)
        rel_part = jnp.dot(
            band_sums(tile_sum, key_block - query_block, span_len),
            band_onehot,
            precision=lax.Precision.HIGHEST,
        )
        return (query_part, key_part, value_part, rel_part)

    query_grad, key_grad, value_grad, rel_grad = tile_grads(
        queries, grad_heads, log_total, row_delta, keys_home, values_home, cycle_place, cycle_place
    )

    def key_turn(cycle_turn, state_now):
        key_rows, value_rows, key_sum, value_sum, query_sum, rel_sum = state_now
        key_sum, value_sum = pass_grads(key_sum, value_sum)
        key_rows, value_rows = from_behind((key_rows, value_rows), "blk", 1)
        source = (cycle_place - cycle_turn) % cycle_size
        query_part, key_part, value_part, rel_part = tile_grads(
            queries, grad_heads, log_total, row_delta, key_rows, value_rows, cycle_place, source
        )
        return (
            key_rows,
            value_rows,
            key_sum + key_part,
            value_sum + value_part,
            query_sum + query_part,
            rel_sum + rel_part,
        )

    state_first = (keys_home, values_home, key_grad, value_grad, query_grad, rel_grad)
    _, _, key_grad, value_grad, query_grad, rel_grad = lax.fori_loop(
        1, cycle_size, key_turn, state_first
    )
    key_grad, value_grad = pass_grads(key_grad, value_grad)
    block_shape = (seq_count, span_len, heads_here * HD)
    query_rows, key_rows_back, value_rows_back = (
        lax.all_to_all(
            query_grad.astype(jnp.bfloat16).reshape(block_shape),
            "head",
            split_axis=1,
            concat_axis=2,
            tiled=True,
        ),
        lax.all_to_all(
            key_grad.astype(jnp.bfloat16).reshape(block_shape),
            "head",
            split_axis=1,
            concat_axis=2,
            tiled=True,
        ),
        lax.all_to_all(
            value_grad.astype(jnp.bfloat16).reshape(block_shape),
            "head",
            split_axis=1,
            concat_axis=2,
            tiled=True,
        ),
    )
    query_rows = query_rows.reshape(-1, HEADS * HD)
    key_rows_back = key_rows_back.reshape(-1, HEADS * HD)
    value_rows_back = value_rows_back.reshape(-1, HEADS * HD)
    grad_query = jnp.dot(first_in.T, query_rows, preferred_element_type=jnp.float32)
    grad_key = jnp.dot(first_in.T, key_rows_back, preferred_element_type=jnp.float32)
    grad_value = jnp.dot(first_in.T, value_rows_back, preferred_element_type=jnp.float32)
    first_grad = (
        jnp.dot(query_rows, back_query.T, preferred_element_type=jnp.float32)
        + jnp.dot(key_rows_back, back_key.T, preferred_element_type=jnp.float32)
        + jnp.dot(value_rows_back, back_value.T, preferred_element_type=jnp.float32)
    )
    input_part, grad_gain_one = norm_one_back(first_grad)
    input_grad = (hidden_grad + input_part).astype(jnp.bfloat16).reshape(inputs.shape)
    rel_full = lax.dynamic_update_slice_in_dim(
        jnp.zeros((HEADS, BUCKETS), jnp.float32), rel_grad, head_place * heads_here, 0
    ).reshape(-1)
    shards = tuple(
        (
            lax.psum_scatter(grad_gain_one, ("head", "blk"), scatter_dimension=0, tiled=True),
            lax.psum_scatter(grad_query, ("head", "blk"), scatter_dimension=0, tiled=True),
            lax.psum_scatter(grad_key, ("head", "blk"), scatter_dimension=0, tiled=True),
            lax.psum_scatter(grad_value, ("head", "blk"), scatter_dimension=0, tiled=True),
            lax.psum_scatter(grad_out, ("head", "blk"), scatter_dimension=0, tiled=True),
            lax.psum_scatter(rel_full, ("head", "blk"), scatter_dimension=0, tiled=True),
            lax.psum_scatter(grad_gain_two, ("head", "blk"), scatter_dimension=0, tiled=True),
            lax.psum_scatter(grad_in, ("head", "blk"), scatter_dimension=0, tiled=True),
            lax.psum_scatter(grad_down, ("head", "blk"), scatter_dimension=0, tiled=True),
        )
    )
    return (
        layer_out,
        input_grad,
        shards[0],
        shards[1],
        shards[2],
        shards[3],
        shards[4],
        shards[5],
        shards[6],
        shards[7],
        shards[8],
    )


TQ = 512
KT = 512
MARGIN = 256
AUG = 80
NT = (((1,), (1,)), ((), ()))


def nn(left, right):
    return jnp.dot(left, right, preferred_element_type=jnp.float32)


def flipped(block):
    return block.astype(jnp.float32).T.astype(jnp.bfloat16)


def ones_row(width):
    first = lax.broadcasted_iota(jnp.int32, (AUG - HD, width), 0) == 0
    return jnp.where(first, 1.0, 0.0).astype(jnp.bfloat16)


def pieces_of(seq_count, part_len, groups):
    for seq in range(seq_count):
        for near in range(2):
            for source in range(groups):
                yield seq, near, source, slice((near * seq_count + seq) * part_len, (near * seq_count + seq + 1) * part_len)


def lanes_of(ref, tile_at, per_tile, part_len, lane_base):
    parts = [ref[tile_at * per_tile + k, :HD, pl.ds(lane_base, part_len)] for k in range(per_tile)]
    return parts[0] if per_tile == 1 else jnp.concatenate(parts, axis=1)


def tile_class(edge_ref, row, key_at, query_at):
    first_start, last_start, first_end, last_end = (edge_ref[row * 4 + k] for k in range(4))
    touched = (key_at + KT > first_start) & (key_at < last_end)
    gap = key_at - query_at
    whole = (key_at >= last_start) & (key_at + KT <= first_end)
    plain = whole & ((gap + KT <= -MAXREL + 1) | (gap >= TQ + MAXREL - 1))
    strip_at = jnp.clip(gap, -(KT + MARGIN), TQ + MARGIN) + KT + MARGIN
    return touched, plain, gap, pl.ds(pl.multiple_of(strip_at, 256), KT)


def masked(scores, bias, key_at, start_row, end_row):
    places = lax.broadcasted_iota(jnp.int32, scores.shape, 0) + key_at
    return jnp.where((places >= start_row) & (places < end_row), scores + bias, FLOOR)


def attend_kernel(chips, base_ref, edge_ref, far_ref, *refs):
    kv_refs, q_ref = refs[:chips], refs[0]
    start_ref, end_ref, bias_ref, o_ref, ob_ref, lse_ref, k_rows, v_aug, top_ref, acc_ref = refs[chips:]
    groups, _, span = q_ref.shape
    blocks, seq_count, span_len, _ = k_rows.shape
    part_len = span_len // groups
    per_tile = TQ // part_len
    tiles, key_tiles = span_len // TQ, span_len // KT
    per_key = KT // part_len
    for far in range(chips):
        for seq, near, source, lanes in pieces_of(seq_count, part_len, groups):
            block = 2 * far + near
            k_rows[block, seq, source * part_len : (source + 1) * part_len, :] = flipped(kv_refs[far][source, HD : 2 * HD, lanes])
            at = source % per_key * part_len
            v_aug[block, seq, source // per_key, :HD, at : at + part_len] = kv_refs[far][source, 2 * HD :, lanes]
    for block in range(blocks):
        for seq in range(seq_count):
            for tile in range(key_tiles):
                v_aug[block, seq, tile, HD:, :] = ones_row(KT)

    for seq in range(seq_count):
        for near in range(2):
            lane_base = (near * seq_count + seq) * part_len

            def query_tile(tile, _, seq=seq, near=near, lane_base=lane_base):
                query_at = base_ref[near] + tile * TQ
                row = (near * seq_count + seq) * tiles + tile
                queries = lanes_of(q_ref, tile, per_tile, part_len, lane_base)
                top_ref[...] = jnp.full_like(top_ref, FLOOR)
                acc_ref[...] = jnp.zeros_like(acc_ref)
                start_row = start_ref[near, seq, pl.ds(tile, 1), :]
                end_row = end_ref[near, seq, pl.ds(tile, 1), :]

                def take(scores, shift, block, key_tile):
                    old_top = top_ref[0:1, :]
                    new_top = jnp.maximum(old_top, jnp.max(scores, axis=0, keepdims=True) + shift)
                    weights = jnp.exp(scores - (new_top - shift))
                    acc_ref[...] = acc_ref[...] * jnp.exp(old_top - new_top) + nn(
                        v_aug[block, seq, key_tile], weights.astype(jnp.bfloat16)
                    )
                    top_ref[0:1, :] = new_top

                def key_step(step, _):
                    block, key_tile = step // key_tiles, step % key_tiles
                    key_at = base_ref[block] + key_tile * KT
                    touched, plain, gap, strip = tile_class(edge_ref, row, key_at, query_at)

                    def raw():
                        keys = k_rows[block, seq, pl.ds(pl.multiple_of(key_tile * KT, KT), KT), :]
                        return nn(keys, queries)

                    @pl.when(touched & plain)
                    def _():
                        take(raw(), jnp.where(gap < 0, far_ref[0], far_ref[1]), block, key_tile)

                    @pl.when(touched & jnp.logical_not(plain))
                    def _():
                        take(masked(raw(), bias_ref[strip, :], key_at, start_row, end_row), 0.0, block, key_tile)

                    return 0

                lax.fori_loop(0, blocks * key_tiles, key_step, 0)
                total = acc_ref[HD : HD + 1, :]
                outs = acc_ref[:HD, :] / total
                lse_ref[near, seq, pl.ds(tile, 1), :] = top_ref[0:1, :] + jnp.log(total)
                for k in range(per_tile):
                    part = outs[:, k * part_len : (k + 1) * part_len]
                    o_ref[tile * per_tile + k, :, lane_base : lane_base + part_len] = part
                    ob_ref[2 * (tile * per_tile + k) + (near ^ base_ref[blocks])] = part.astype(jnp.bfloat16)
                return 0

            lax.fori_loop(0, tiles, query_tile, 0)


def attend_back_kernel(chips, carried, g_base, base_ref, edge_ref, far_ref, g_ref, o_ref, lse_ref, *refs):
    kv_refs, q_ref, refs = refs[:chips], refs[0], refs[chips:]
    start_ref, end_ref, bias_ref, *refs = refs
    if carried:
        old_band_ref, old_sides_ref, *refs = refs
    made_refs, refs = refs[:chips], refs[chips:]
    dq_ref = made_refs[0]
    band_ref, sides_ref, k_rows, v_rows, k_aug, dk_acc, dv_acc, dq_acc = refs
    groups, _, span = q_ref.shape
    blocks, seq_count, span_len, _ = k_rows.shape
    part_len = span_len // groups
    per_tile = TQ // part_len
    tiles, key_tiles = span_len // TQ, span_len // KT
    per_key = KT // part_len
    for far in range(chips):
        for seq, near, source, lanes in pieces_of(seq_count, part_len, groups):
            block = 2 * far + near
            rows = slice(source * part_len, (source + 1) * part_len)
            piece = kv_refs[far][source, HD : 2 * HD, lanes]
            k_rows[block, seq, rows, :] = flipped(piece)
            v_rows[block, seq, rows, :] = flipped(kv_refs[far][source, 2 * HD :, lanes])
            at = source % per_key * part_len
            k_aug[block, seq, source // per_key, :HD, at : at + part_len] = piece
    for block in range(blocks):
        for seq in range(seq_count):
            for tile in range(key_tiles):
                k_aug[block, seq, tile, HD:, :] = ones_row(KT)
    dk_acc[...] = jnp.zeros_like(dk_acc)
    dv_acc[...] = jnp.zeros_like(dv_acc)
    band_ref[...] = old_band_ref[...] if carried else jnp.zeros_like(band_ref)
    sides_ref[...] = old_sides_ref[...] if carried else jnp.zeros_like(sides_ref)

    for seq in range(seq_count):
        for near in range(2):
            lane_base = (near * seq_count + seq) * part_len

            def query_tile(tile, _, seq=seq, near=near, lane_base=lane_base):
                query_at = base_ref[near] + tile * TQ
                row = (near * seq_count + seq) * tiles + tile
                queries = lanes_of(q_ref, tile, per_tile, part_len, lane_base)
                first = 2 * tile * per_tile + (near ^ base_ref[blocks])
                grads = [g_ref[first + 2 * k, :, g_base : g_base + part_len] for k in range(per_tile)]
                grads = jnp.concatenate(grads, axis=1)
                outs = lanes_of(o_ref, tile, per_tile, part_len, lane_base)
                delta = jnp.sum(grads.astype(jnp.float32) * outs, axis=0, keepdims=True)
                query_rows, grad_rows = flipped(queries), flipped(grads)
                lse = lse_ref[near, seq, pl.ds(tile, 1), :]
                start_row = start_ref[near, seq, pl.ds(tile, 1), :]
                end_row = end_ref[near, seq, pl.ds(tile, 1), :]
                dq_acc[...] = jnp.zeros_like(dq_acc)

                def take(scores, shift, block, key_tile):
                    rows = pl.ds(pl.multiple_of(key_tile * KT, KT), KT)
                    probs = jnp.exp(scores - (lse - shift))
                    score_grad = probs * (nn(v_rows[block, seq, rows, :], grads) - delta)
                    score_low = score_grad.astype(jnp.bfloat16)
                    dv_acc[block, seq, rows, :] += nn(probs.astype(jnp.bfloat16), grad_rows)
                    dk_acc[block, seq, rows, :] += nn(score_low, query_rows)
                    made = nn(k_aug[block, seq, key_tile], score_low)
                    dq_acc[...] += made
                    return score_grad, made[HD : HD + 1, :]

                def key_step(step, _):
                    block, key_tile = step // key_tiles, step % key_tiles
                    key_at = base_ref[block] + key_tile * KT
                    touched, plain, gap, strip = tile_class(edge_ref, row, key_at, query_at)

                    def raw():
                        keys = k_rows[block, seq, pl.ds(pl.multiple_of(key_tile * KT, KT), KT), :]
                        return nn(keys, queries)

                    @pl.when(touched & plain)
                    def _():
                        _, sums = take(raw(), jnp.where(gap < 0, far_ref[0], far_ref[1]), block, key_tile)
                        side = (gap > 0).astype(jnp.int32)
                        sides_ref[pl.ds(side, 1), :] += sums

                    @pl.when(touched & jnp.logical_not(plain))
                    def _():
                        whole_grad, _ = take(
                            masked(raw(), bias_ref[strip, :], key_at, start_row, end_row), 0.0, block, key_tile
                        )
                        band_ref[strip, :] += whole_grad

                    return 0

                lax.fori_loop(0, blocks * key_tiles, key_step, 0)
                for k in range(per_tile):
                    part = dq_acc[:HD, k * part_len : (k + 1) * part_len].astype(jnp.bfloat16)
                    dq_ref[tile * per_tile + k, :HD, lane_base : lane_base + part_len] = part
                return 0

            lax.fori_loop(0, tiles, query_tile, 0)
    for far in range(chips):
        for seq, near, source, lanes in pieces_of(seq_count, part_len, groups):
            block = 2 * far + near
            rows = slice(source * part_len, (source + 1) * part_len)
            top = 0 if far else HD
            made_refs[far][source, top : top + HD, lanes] = dk_acc[block, seq, rows, :].T.astype(jnp.bfloat16)
            made_refs[far][source, top + HD : top + 2 * HD, lanes] = dv_acc[block, seq, rows, :].T.astype(jnp.bfloat16)


def strip_places():
    width = TQ + 128
    lane = np.arange(width)
    lane = np.where(lane < TQ, lane, lane - width)
    offset = 128 * (np.arange(TQ // 128 + 2)[:, None] - 1) - lane[None, :]
    return np.clip(offset, -MAXREL, MAXREL) + MAXREL


def strip_kernel(far_ref, wave_ref, strip_ref):
    near_blocks, _, width = wave_ref.shape
    first = KT + MARGIN - 128
    strip_ref[:first, :] = jnp.full((first, TQ), far_ref[0], jnp.float32)
    for k in range(near_blocks):
        spread = jnp.broadcast_to(wave_ref[k], (128, width))
        turned = pltpu.roll(spread, 0, 1, stride=1, stride_axis=0)
        strip_ref[first + 128 * k : first + 128 * (k + 1), :] = turned[:, :TQ]
    last = first + 128 * near_blocks
    strip_ref[last:, :] = jnp.full((strip_ref.shape[0] - last, TQ), far_ref[1], jnp.float32)


def bias_strip(far_bias, waves):
    return pl.pallas_call(
        strip_kernel,
        name="bias_strip",
        out_shape=jax.ShapeDtypeStruct((2 * KT + 2 * MARGIN + TQ, TQ), jnp.float32),
        in_specs=[SMEM, VMEM],
        out_specs=VMEM,
        compiler_params=pltpu.CompilerParams(vmem_limit_bytes=32 * 2**20),
    )(far_bias, waves)


def band_kernel(band_ref, sides_ref, near_ref, far_ref):
    near_blocks, _, width = near_ref.shape
    first = KT + MARGIN - 128
    last = first + 128 * near_blocks
    left = jnp.sum(band_ref[:first, :], axis=0, keepdims=True) + sides_ref[0:1, :]
    right = jnp.sum(band_ref[last:, :], axis=0, keepdims=True) + sides_ref[1:2, :]
    far_ref[...] = jnp.concatenate([left, right, jnp.zeros((6, TQ), jnp.float32)], axis=0)
    for k in range(near_blocks):
        rows = band_ref[first + 128 * k : first + 128 * (k + 1), :]
        spread = jnp.concatenate([rows, jnp.zeros((128, width - TQ), jnp.float32)], axis=1)
        row = lax.broadcasted_iota(jnp.int32, spread.shape, 0)
        for step in (1, 2, 4):
            spread = jnp.where((row & step) != 0, pltpu.roll(spread, width - step, 1), spread)
        total = spread[:8, :]
        for at in range(8, 128, 8):
            total = total + pltpu.roll(spread[at : at + 8, :], width - at, 1)
        near_ref[k] = jnp.sum(total, axis=0, keepdims=True)


def band_sums_of(band, sides):
    return pl.pallas_call(
        band_kernel,
        name="band_sums",
        out_shape=(
            jax.ShapeDtypeStruct((TQ // 128 + 2, 1, TQ + 128), jnp.float32),
            jax.ShapeDtypeStruct((8, TQ), jnp.float32),
        ),
        in_specs=[VMEM, VMEM],
        out_specs=(VMEM, VMEM),
        compiler_params=pltpu.CompilerParams(vmem_limit_bytes=32 * 2**20),
    )(band, sides)


SMEM = pl.BlockSpec(memory_space=pltpu.SMEM)
VMEM = pl.BlockSpec(memory_space=pltpu.VMEM)


def attend(base, edges, far_bias, kvs, starts, ends, bias):
    chips = len(kvs)
    groups, _, span = kvs[0].shape
    shape = (groups, HD, span)
    _, seq_count, tiles, _ = starts.shape
    blocks, span_len = 2 * chips, tiles * TQ
    return pl.pallas_call(
        functools.partial(attend_kernel, chips),
        name="attend",
        out_shape=(
            jax.ShapeDtypeStruct(shape, jnp.float32),
            jax.ShapeDtypeStruct((2 * groups, HD, span // 2), jnp.bfloat16),
            jax.ShapeDtypeStruct(starts.shape, jnp.float32),
        ),
        in_specs=[SMEM] * 3 + [VMEM] * (chips + 3),
        out_specs=(VMEM,) * 3,
        scratch_shapes=[
            pltpu.VMEM((blocks, seq_count, span_len, HD), jnp.bfloat16),
            pltpu.VMEM((blocks, seq_count, span_len // KT, AUG, KT), jnp.bfloat16),
            pltpu.VMEM((8, TQ), jnp.float32),
            pltpu.VMEM((AUG, TQ), jnp.float32),
        ],
        cost_estimate=pl.CostEstimate(flops=1, transcendentals=0, bytes_accessed=1),
        compiler_params=pltpu.CompilerParams(vmem_limit_bytes=48 * 2**20),
    )(base, edges, far_bias, *kvs, starts, ends, bias)


def attend_back(base, edges, far_bias, g, seq, o, lse, kvs, starts, ends, bias, sums=()):
    chips = len(kvs)
    groups, _, span = kvs[0].shape
    _, seq_count, tiles, _ = starts.shape
    blocks, span_len = 2 * chips, tiles * TQ
    made = pl.pallas_call(
        functools.partial(attend_back_kernel, chips, bool(sums), seq * span // 2),
        name="attend_back",
        out_shape=(jax.ShapeDtypeStruct(kvs[0].shape, jnp.bfloat16),)
        + (jax.ShapeDtypeStruct((groups, 2 * HD, span), jnp.bfloat16),) * (chips - 1)
        + (jax.ShapeDtypeStruct(bias.shape, jnp.float32), jax.ShapeDtypeStruct((8, TQ), jnp.float32)),
        in_specs=[SMEM] * 3
        + [VMEM] * (3 + chips + 3 + len(sums)),
        out_specs=(VMEM,) * (2 + chips),
        scratch_shapes=[
            pltpu.VMEM((blocks, seq_count, span_len, HD), jnp.bfloat16),
            pltpu.VMEM((blocks, seq_count, span_len, HD), jnp.bfloat16),
            pltpu.VMEM((blocks, seq_count, span_len // KT, AUG, KT), jnp.bfloat16),
            pltpu.VMEM((blocks, seq_count, span_len, HD), jnp.float32),
            pltpu.VMEM((blocks, seq_count, span_len, HD), jnp.float32),
            pltpu.VMEM((AUG, TQ), jnp.float32),
        ],
        cost_estimate=pl.CostEstimate(flops=1, transcendentals=0, bytes_accessed=1),
        compiler_params=pltpu.CompilerParams(vmem_limit_bytes=56 * 2**20),
    )(base, edges, far_bias, g, o, lse, *kvs, starts, ends, bias, *sums)
    return made[0], made[1:chips], made[-2:]


def trade(block, axis, bit):
    size = lax.axis_size(axis)
    return lax.ppermute(block, axis, [(i, i ^ bit) for i in range(size)])


def mate(block):
    return trade(block, "blk", 1)


def across_x(block):
    return trade(block, "blk", 2)


def across_y(block):
    return trade(block, "head", 1)


def across_z(block, distance):
    return trade(block, "head", 2 * distance)


def whole_block(array):
    return pl.BlockSpec(array.shape, lambda i: (0,) * len(array.shape))


def copy_kernel(plan, slots_ref, *arrays):
    for source, source_rows, target, target_rows, count in plan:
        views = []
        for which, (slot, scale, first, columns) in ((source, source_rows), (target, target_rows)):
            begin = first if slot is None else pl.multiple_of(slots_ref[slot] * scale, 8) + first
            views.append(arrays[which].at[pl.ds(begin, count), pl.ds(columns[0], columns[1])])
        views[1][...] = views[0][...]


def moved(name, slots, sources, shapes, plan):
    outs = tuple(pltpu.HBM(shape, sources[0].dtype) for shape in shapes)
    return pl.pallas_call(
        functools.partial(copy_kernel, plan),
        name=name,
        grid=(1,),
        out_shape=outs,
        in_specs=[SMEM] + [whole_block(block) for block in sources],
        out_specs=tuple(whole_block(block) for block in outs),
        compiler_params=pltpu.CompilerParams(vmem_limit_bytes=48 * 2**20),
    )(slots, *sources)


DEPTH = 4
CHIPS = 16


def turn_of(k):
    return k % DEPTH, k // DEPTH // 2, k // DEPTH % 2


def slot_table():
    n_blk = lax.axis_size("blk")
    group, place = lax.axis_index("head"), lax.axis_index("blk")
    groups = group ^ jnp.asarray([2 * turn_of(k)[0] + turn_of(k)[1] for k in range(CHIPS)], jnp.int32)
    sides = (place // 2) ^ jnp.asarray([turn_of(k)[2] for k in range(CHIPS)], jnp.int32)
    chips = groups * (n_blk // 2) + sides
    return jnp.concatenate([chips, groups, 2 * chips + place % 2, 2 * chips + 1 - place % 2])


CHIP, GROUP, DEVICE, MATE = 0, CHIPS, 2 * CHIPS, 3 * CHIPS


def after(block, *earlier):
    return lax.optimization_barrier((block, earlier))[0]


def beside(made, *sent):
    return lax.optimization_barrier((made, *sent))


def wide(block):
    return block.astype(jnp.float32)


def placed(name, slots, blocks, layout, shapes, order):
    plan = []
    for k, (which, at) in enumerate(order):
        for first, count, whole, take, target in layout:
            plan.append((which, (None, 0, at + first, take), len(blocks) + whole, target(k), count))
    return moved(name, slots, blocks, shapes, tuple(plan))


def parted(name, slots, wholes, layout, shapes, order):
    plan = []
    for k, (which, at) in enumerate(order):
        for first, count, whole, take, target in layout:
            plan.append((whole, target(k), len(wholes) + which, (None, 0, at + first, take), count))
    return moved(name, slots, wholes, shapes, tuple(plan))


def grouped(rows):
    order = []
    for k in range(CHIPS):
        group, z = k // DEPTH, k % DEPTH
        order.append((group, z * rows) if group < 3 else (3 + z // 2, z % 2 * rows))
    return order


def gather_z(payload, *earlier):
    payload = after(payload, *earlier) if earlier else payload
    return [payload] + [across_z(payload, k) for k in range(1, DEPTH)]


def gather_xy(own, *earlier):
    own = jnp.concatenate(own, axis=0)
    own = after(own, *earlier) if earlier else own
    return own, across_x(own), across_y(own)


def gather_corner(blocks, *earlier):
    own, by_x, by_y = blocks
    half = own.shape[0] // 2
    low, high = by_x[:half], by_y[half:]
    if earlier:
        low, high = after(low, *earlier), after(high, *earlier)
    return own, by_x, by_y, across_y(low), across_x(high)


def sum_parts(name, slots, wholes, layout, rows, width):
    full, half = DEPTH * rows, DEPTH // 2 * rows
    shapes = ((full, width),) * 3 + ((half, width),) * 2
    return parted(name, slots, wholes, layout, shapes, grouped(rows))


def sum_corner(blocks):
    own, by_x, by_y, low, high = blocks
    return own, by_x, by_y, across_y(low), across_x(high)


def sum_xy(blocks):
    own, by_x, by_y, low, high = blocks
    half = low.shape[0]
    return own, across_x(added(by_x, low, slice(0, half))), across_y(added(by_y, high, slice(half, 2 * half)))


def column_kernel(*refs):
    groups, outs = refs[:-DEPTH], refs[-DEPTH:]
    first = 0
    for at in range(0, len(groups), 3):
        rows = groups[at].shape[0] // DEPTH
        for k, out_ref in enumerate(outs):
            here = slice(k * rows, (k + 1) * rows)
            total = sum(wide(ref[here]) for ref in groups[at : at + 3])
            out_ref[first : first + rows, :] = total.astype(out_ref.dtype)
        first += rows


def column_sent(*groups):
    rows, width = sum(group[0].shape[0] for group in groups) // DEPTH, groups[0][0].shape[1]
    blocks = [block for group in groups for block in group]
    here, *given = pl.pallas_call(
        column_kernel,
        name="column",
        out_shape=[jax.ShapeDtypeStruct((rows, width), jnp.float32)]
        + [jax.ShapeDtypeStruct((rows, width), jnp.bfloat16)] * (DEPTH - 1),
        in_specs=[VMEM] * len(blocks),
        out_specs=[VMEM] * DEPTH,
        compiler_params=pltpu.CompilerParams(vmem_limit_bytes=32 * 2**20),
    )(*blocks)
    return [here] + [across_z(block, k + 1) for k, block in enumerate(given)]


def column_total(blocks):
    here, *met = blocks
    return here + sum(wide(block) for block in met)


def norm_kernel(here_ref, there_ref, gain_ref, rows_ref, scale_ref, *normed_refs):
    seqs, part, _ = here_ref.shape
    for seq in range(seqs):
        for which, ref in enumerate((here_ref, there_ref)):
            rows = wide(ref[seq])
            scale = lax.rsqrt(jnp.mean(rows * rows, axis=-1, keepdims=True) + EPS)
            normed = (rows * scale * gain_ref[...]).astype(here_ref.dtype)
            normed_refs[seq][which * part : (which + 1) * part, :] = normed
            if which == 0:
                rows_ref[seq * part : (seq + 1) * part, :] = rows
                scale_ref[seq * part : (seq + 1) * part, :] = scale


def normed_by_seq(here, there, gain):
    seqs, part, width = here.shape
    shapes = [(seqs * part, width), (seqs * part, 1)]
    return pl.pallas_call(
        norm_kernel,
        name="normed_by_seq",
        out_shape=[jax.ShapeDtypeStruct(shape, jnp.float32) for shape in shapes]
        + [jax.ShapeDtypeStruct((2 * part, width), here.dtype)] * seqs,
        in_specs=[VMEM] * 3,
        out_specs=[VMEM] * (2 + seqs),
    )(here, there, gain.reshape(1, width))


def feed_kernel(rows_ref, grad_ref, in_ref, down_ref, act_ref, up_ref, out_near, out_far, back_near, back_far):
    half = rows_ref.shape[0] // 2
    values, rise = gelu_both(nn(rows_ref[...], in_ref[...]))
    values = values.astype(act_ref.dtype)
    act_ref[...] = values
    up = (dot_on(grad_ref[...], down_ref[...], 1, 1) * rise).astype(up_ref.dtype)
    up_ref[...] = up
    made, back = nn(values, down_ref[...]), dot_on(up, in_ref[...], 1, 1)
    parts = ((out_near, made[:half]), (out_far, made[half:]), (back_near, back[:half]), (back_far, back[half:]))

    @pl.when(pl.program_id(0) == 0)
    def _():
        for ref, part in parts:
            ref[...] = part

    @pl.when(pl.program_id(0) > 0)
    def _():
        for ref, part in parts:
            ref[...] += part


def feed(rows, grads, in_w, down_w):
    tokens, width = rows.shape
    hidden, step = in_w.shape[1], 512
    whole = pl.BlockSpec((tokens, width), lambda i: (0, 0))
    half = pl.BlockSpec((tokens // 2, width), lambda i: (0, 0))
    units = pl.BlockSpec((tokens, step), lambda i: (0, i))
    return pl.pallas_call(
        feed_kernel,
        name="feed",
        grid=(hidden // step,),
        out_shape=[pltpu.HBM((tokens, hidden), rows.dtype)] * 2
        + [pltpu.HBM((tokens // 2, width), jnp.float32)] * 4,
        in_specs=[
            whole,
            whole,
            pl.BlockSpec((width, step), lambda i: (0, i)),
            pl.BlockSpec((step, width), lambda i: (i, 0)),
        ],
        out_specs=[units] * 2 + [half] * 4,
        cost_estimate=pl.CostEstimate(flops=1, transcendentals=0, bytes_accessed=1),
        compiler_params=pltpu.CompilerParams(vmem_limit_bytes=32 * 2**20),
    )(rows, grads, in_w, down_w)


def weight_grad_kernel(left_ref, right_ref, out_ref):
    out_ref[...] = dot_on(left_ref[...], right_ref[...], 0, 0).astype(out_ref.dtype)


def weight_grad(left, right):
    tokens, rows = left.shape
    cols, step = right.shape[1], 512
    left, right = (pltpu.with_memory_space_constraint(block, pltpu.HBM) for block in (left, right))
    return pl.pallas_call(
        weight_grad_kernel,
        name="weight_grad",
        grid=(rows // step,),
        out_shape=jax.ShapeDtypeStruct((rows, cols), left.dtype),
        in_specs=[pl.BlockSpec((tokens, step), lambda i: (0, i)), pl.BlockSpec((tokens, cols), lambda i: (0, 0))],
        out_specs=pl.BlockSpec((step, cols), lambda i: (i, 0)),
        cost_estimate=pl.CostEstimate(flops=1, transcendentals=0, bytes_accessed=1),
        compiler_params=pltpu.CompilerParams(vmem_limit_bytes=32 * 2**20),
    )(left, right)


def first_back_kernel(plan, slots_ref, in_0, made_0, in_1, made_1, *refs):
    *parts, whole_ref = refs
    rows = whole_ref.shape[0]
    step = 256
    for at in range(0, rows, step):
        here = slice(at, at + step)
        product = dot_on(in_0[here], made_0[...], 1, 1) + dot_on(in_1[here], made_1[...], 1, 1)
        whole_ref[here, :] = product.astype(whole_ref.dtype)
    for slot, scale, which, at in plan:
        source = pl.ds(pl.multiple_of(slots_ref[slot] * scale, scale), scale)
        parts[which][at : at + scale, :] = whole_ref[source, :]


def first_back(slots, plan, shapes, ins, made):
    outs = [pltpu.HBM(shape, made[0].dtype) for shape in shapes]
    sources = (ins[0], made[0], ins[1], made[1])
    sources = [pltpu.with_memory_space_constraint(block, pltpu.HBM) for block in sources]
    return pl.pallas_call(
        functools.partial(first_back_kernel, plan),
        name="first_back",
        grid=(1,),
        out_shape=outs,
        in_specs=[SMEM] + [whole_block(block) for block in sources],
        out_specs=[whole_block(block) for block in outs],
        scratch_shapes=[pltpu.VMEM((ins[0].shape[0], made[0].shape[0]), made[0].dtype)],
        compiler_params=pltpu.CompilerParams(vmem_limit_bytes=48 * 2**20),
    )(slots, *sources)


def last_kernel(first_ref, second_ref, wq_ref, wk_ref, wv_ref, q_ref, k_ref, v_ref, gain_ref):
    groups = first_ref.shape[1] // (3 * HD)
    for g in range(groups):
        for which, out_ref in enumerate((q_ref, k_ref, v_ref)):
            at = (3 * g + which) * HD
            pair = [ref[:, at : at + HD] for ref in (first_ref, second_ref)]
            out_ref[:, 2 * g * HD : 2 * (g + 1) * HD] = jnp.concatenate(pair, axis=1)
    products = sum(wide(w[...]) * grad[...] for w, grad in ((wq_ref, q_ref), (wk_ref, k_ref), (wv_ref, v_ref)))
    gain_ref[...] = jnp.sum(products, axis=1, keepdims=True)


def by_weight(first, second, *weights):
    rows, width = weights[0].shape
    return pl.pallas_call(
        last_kernel,
        name="by_weight",
        out_shape=[jax.ShapeDtypeStruct((rows, width), jnp.float32)] * 3 + [jax.ShapeDtypeStruct((rows, 1), jnp.float32)],
        in_specs=[VMEM] * 5,
        out_specs=[VMEM] * 4,
    )(first, second, *weights)


def halves_kernel(place_ref, in_ref, out_ref, *refs):
    *down_refs, in_w_ref, out_w_ref, down_w_ref = refs
    devices, rows, width = out_ref.shape
    for d in range(devices):
        here = pl.ds(d * rows, rows)
        for j in range(in_ref.shape[1] // rows):
            in_w_ref[here, j * width : (j + 1) * width] = in_ref[d, j * rows : (j + 1) * rows, :]
        out_w_ref[here, :] = out_ref[d]
    rows = down_refs[0].shape[1]
    for chip, down_ref in enumerate(down_refs):
        down_w_ref[pl.ds(chip * rows, rows), :] = down_ref[0]


def own_halves(core, whole, down_rows, shard):
    devices, rows, width = whole.shape
    steps, chips = 4, devices // 2
    in_rows = (rows - down_rows - shard) // 2
    in_at, out_at = down_rows // in_rows, (rows - shard) // shard
    shapes = (
        (devices * shard, in_rows // shard * width),
        (devices * shard, width),
        (chips * down_rows, width),
    )
    return pl.pallas_call(
        halves_kernel,
        name="own_halves",
        grid_spec=pltpu.PrefetchScalarGridSpec(
            num_scalar_prefetch=1,
            grid=(steps,),
            in_specs=[
                pl.BlockSpec((devices // steps, in_rows, width), lambda i, place_ref: (i, in_at + place_ref[0], 0)),
                pl.BlockSpec((devices // steps, shard, width), lambda i, place_ref: (i, out_at, 0)),
            ]
            + [
                pl.BlockSpec(
                    (1, down_rows, width), lambda i, place_ref, j=j: (2 * (i * chips // steps + j) + place_ref[0], 0, 0)
                )
                for j in range(chips // steps)
            ],
            out_specs=[pl.BlockSpec((shape[0] // steps, shape[1]), lambda i, place_ref: (i, 0)) for shape in shapes],
        ),
        out_shape=[pltpu.HBM(shape, whole.dtype) for shape in shapes],
        compiler_params=pltpu.CompilerParams(vmem_limit_bytes=32 * 2**20),
    )(core.reshape(1), *[whole] * (2 + chips // steps))


def add_kernel(place, whole_ref, part_ref, sum_ref):
    sum_ref[...] = whole_ref[...]
    sum_ref[place] = (wide(whole_ref[place]) + wide(part_ref[...])).astype(sum_ref.dtype)


def added(whole, part, place):
    return pl.pallas_call(
        functools.partial(add_kernel, place),
        name="added",
        out_shape=jax.ShapeDtypeStruct(whole.shape, whole.dtype),
        in_specs=[VMEM] * 2,
        out_specs=VMEM,
        compiler_params=pltpu.CompilerParams(vmem_limit_bytes=32 * 2**20),
    )(whole, part)


def document_bounds(segments):
    seq_count, blocks, span_len = segments.shape
    length = blocks * span_len
    numbers = lax.iota(jnp.int32, length // min(512, length) + 2)
    flat = segments.reshape(seq_count, length)
    below = jnp.sum((flat[:, :, None] < numbers).astype(jnp.int32), axis=1)
    here = flat[:, :, None] == numbers[:-1]
    starts = jnp.sum(jnp.where(here, below[:, None, :-1], 0), axis=2)
    ends = jnp.sum(jnp.where(here, below[:, None, 1:], 0), axis=2)
    return starts.reshape(segments.shape), ends.reshape(segments.shape)


def query_bounds(bounds, place, tile):
    near = [lax.dynamic_index_in_dim(bounds, place ^ k, 1, keepdims=False) for k in (0, 2)]
    near = jnp.stack(near, axis=0)
    return near.reshape(near.shape[0], near.shape[1], -1, tile)


def gelu_both(values):
    slope = float(np.sqrt(2.0 / np.pi))
    square = values * values
    curve = jnp.tanh(slope * values * (1.0 + 0.044715 * square))
    half = 0.5 * (1.0 + curve)
    rise = half + 0.5 * values * (1.0 - curve * curve) * (slope * (1.0 + 3 * 0.044715 * square))
    return values * half, rise


def joined(block):
    return jnp.concatenate([block, mate(block)], axis=0)


def halves_added(block):
    half = block.shape[0] // 2
    return block[:half] + mate(block[half:])


def norm_back(grad, rows, scale, gain):
    weighted = grad * gain
    inner = jnp.mean(rows * weighted, axis=-1, keepdims=True)
    return scale * weighted - rows * (scale * scale * scale) * inner


def dot_on(left, right, left_dim, right_dim):
    return lax.dot_general(left, right, (((left_dim,), (right_dim,)), ((), ())), preferred_element_type=jnp.float32)


def pair_body(
    inputs,
    segments,
    bucket_table,
    norm_gain,
    w_query,
    w_key,
    w_value,
    w_out,
    rel_bias,
    ff_gain,
    w_in,
    w_down,
    cotangent,
):
    low = jnp.bfloat16
    seq_count, _, part_len, width = inputs.shape
    groups = lax.axis_size("head")
    span_len = part_len * groups
    blocks = lax.axis_size("blk")
    group, place = lax.axis_index("head"), lax.axis_index("blk")
    core, side = place % 2, place // 2
    slots = slot_table()
    shard = w_query.shape[0]
    chip_rows = 2 * shard
    head_cols = 3 * HD
    first_cols = groups * head_cols
    half_width = groups * HD
    half_hidden = w_in.shape[1] // 2
    down_rows = w_down.shape[0]
    tokens = seq_count * part_len

    def all_rows(pieces):
        return jnp.concatenate(pieces, axis=0)

    turned = segments[1, -1, -1] < segments[0, -1, -1]

    def in_order(block):
        return jnp.where(turned, block[::-1], block)

    inputs, cotangent, segments = in_order(inputs), in_order(cotangent), in_order(segments)

    def by_core(first, second):
        return jnp.where(core == 0, first, second)

    def by_side(first, second):
        return jnp.where(side == 0, first, second)

    cores = [[g * blocks + 2 * s + c for g in range(groups) for s in range(blocks // 2)] for c in range(2)]

    def exchanged_all(block):
        return lax.all_to_all(block, ("head", "blk"), split_axis=0, concat_axis=0, tiled=True, axis_index_groups=cores)

    def exchanged(block):
        return lax.all_to_all(block, "head", split_axis=0, concat_axis=0, tiled=True)

    every, first_every = (0, width), (0, first_cols)
    def head_columns(weight, which):
        return weight.reshape(shard, groups, 2, HD)[:, :, which]

    def cut(which):
        return jnp.stack([head_columns(w, which) for w in (w_query, w_key, w_value)], axis=2).reshape(shard, -1)

    first_cut, second_cut = cut(0), cut(1)
    chunks = [by_side(first_cut, second_cut), across_x(by_side(second_cut, first_cut))]
    gains = jnp.concatenate([norm_gain, ff_gain, rel_bias, jnp.zeros((128 - 5 * shard // 2,), low)])
    gains = jnp.broadcast_to(jnp.pad(gains[None, :], ((0, 7), (0, 0))), (2 * CHIPS, 8, 128))
    gain_w = lax.all_to_all(after(gains, chunks[1]), ("head", "blk"), split_axis=0, concat_axis=0, tiled=True)
    gain_w = wide(gain_w[:, 0])
    gain_one = gain_w[:, :shard].reshape(-1)
    gain_two = gain_w[:, shard : 2 * shard].reshape(-1)

    input_rows = inputs.reshape(seq_count, part_len, width)
    token_rows, scale_one, *first_in = normed_by_seq(input_rows, across_x(input_rows), gain_one)

    first_blocks = []
    for at, chunk in enumerate(chunks):
        own = jnp.concatenate(gather_z(chunk), axis=0)
        if at == 0:
            own, chunks[1] = beside(own, chunks[1])
        by_y = across_y(own)
        if at == 1:
            by_y, first_in = beside(by_y, first_in)
        both = jnp.concatenate([own, by_y], axis=0)
        first_blocks += [both, mate(both)]
    plan = []
    for k in range(CHIPS):
        z, y, x = turn_of(k)
        for far, slot in enumerate((DEVICE, MATE)):
            source = (None, 0, (DEPTH * y + z) * shard, first_every)
            plan.append((2 * x + far, source, 4, (slot + k, shard, 0, first_every), shard))
    (first_w,) = moved("whole_first", slots, first_blocks, ((width, first_cols),), tuple(plan))

    def hidden_columns(which):
        return w_in.reshape(shard, -1, 2, down_rows)[:, :, which].reshape(shard, -1, width)

    payload_in = jnp.stack([hidden_columns(0), hidden_columns(1)], axis=0).transpose(0, 2, 1, 3).reshape(-1, width)
    in_rows = 2 * chip_rows + shard
    payload = jnp.concatenate([w_down, payload_in, w_out], axis=0)
    whole = lax.all_gather(payload, ("head", "blk"), axis=0, tiled=False)
    whole = pltpu.with_memory_space_constraint(whole, pltpu.HBM)

    lay_in = (
        (0, chip_rows, 0, every, lambda k: (CHIP + k, chip_rows, 0, (0, width))),
        (chip_rows, chip_rows, 0, every, lambda k: (CHIP + k, chip_rows, 0, (width, width))),
        (2 * chip_rows, shard, 1, every, lambda k: (CHIP + k, shard, 0, every)),
    )
    lay_down = ((0, down_rows, 0, every, lambda k: (CHIP + k, down_rows, 0, every)),)

    rel_table = gain_w[:, 2 * shard : 5 * shard // 2].reshape(HEADS, BUCKETS)
    rel_here = lax.dynamic_index_in_dim(rel_table, 2 * group + side, 0, keepdims=False)

    bucket_hot = bucket_table[:, None] == lax.iota(jnp.int32, BUCKETS)[None, :]
    by_offset = jnp.sum(jnp.where(bucket_hot, rel_here[None, :], 0.0), axis=1)
    places = strip_places()
    place_hot = jnp.asarray(places.reshape(-1))[:, None] == lax.iota(jnp.int32, 2 * MAXREL + 1)[None, :]
    place_hot = place_hot.astype(jnp.float32)
    waves = jnp.dot(place_hot, by_offset, precision=lax.Precision.HIGHEST)
    waves = waves.reshape(places.shape[0], 1, places.shape[1])
    far_bias = jnp.stack([by_offset[0], by_offset[-1]])
    bias = bias_strip(far_bias, waves)
    starts, ends = document_bounds(segments)
    starts, ends = query_bounds(starts, place, TQ), query_bounds(ends, place, TQ)
    edges = jnp.stack([starts[..., 0], starts[..., -1], ends[..., 0], ends[..., -1]], axis=-1)
    base = (place ^ jnp.asarray([0, 2, 1, 3], jnp.int32)) * span_len
    base = jnp.concatenate([base, side.reshape(1)])

    made = [dot_on(first_w, rows, 0, 1).astype(low) for rows in first_in]
    sent = exchanged(made[0].reshape(groups, head_cols, 2 * part_len))
    sent, bias, far_bias, starts, ends, edges = beside(sent, bias, far_bias, starts, ends, edges)
    bounds = [(starts[:, seq : seq + 1], ends[:, seq : seq + 1], bias) for seq in range(seq_count)]
    edges = [edges[:, seq].reshape(-1) for seq in range(seq_count)]
    attended, heads, attn_cols = [], [], [None] * seq_count
    for seq in range(seq_count):
        heads.append([sent, mate(sent)])
        if seq + 1 < seq_count:
            heads[seq][1], made[seq + 1] = beside(heads[seq][1], made[seq + 1])
        done = attend(base, edges[seq], far_bias, heads[seq], *bounds[seq])
        if seq + 1 < seq_count:
            done, sent = beside(done, exchanged(made[seq + 1].reshape(groups, head_cols, 2 * part_len)))
        else:
            done, attn_cols[seq - 1] = beside(done, attn_cols[seq - 1])
        attended.append(done)
        attn_cols[seq] = exchanged_all(done[1])
    attn_cols[1], in_w, out_w, down_w = beside(attn_cols[1], *own_halves(core, whole, down_rows, shard))
    attn_cols = jnp.concatenate([block.reshape(2 * half_width, part_len) for block in attn_cols], axis=1)
    hidden_one = token_rows + dot_on(attn_cols, out_w, 0, 0)
    scale_two = lax.rsqrt(jnp.mean(hidden_one * hidden_one, axis=-1, keepdims=True) + EPS)
    second_in = joined((hidden_one * scale_two * gain_two).astype(low))
    incoming_low = cotangent.reshape(tokens, width)
    incoming = joined(incoming_low)
    activated, up_grad, layer_near, layer_far, back_near, back_far = feed(second_in, incoming, in_w, down_w)
    whole_down = weight_grad(activated, incoming)
    down_parts = sum_parts("parts_down", slots, (whole_down,), lay_down, down_rows, width)
    down_parts = sum_corner(down_parts)
    second_grad = back_near + mate(back_far)
    hidden_part = norm_back(second_grad, hidden_one, scale_two, gain_two)
    hidden_grad = wide(incoming_low) + hidden_part
    branch = hidden_grad.astype(low)
    grads = dot_on(out_w, branch, 1, 1).astype(low).reshape(HEADS, HD, tokens)
    late_in, late_branch = after((second_in, branch), grads, down_parts)
    whole_in = weight_grad(late_in, up_grad)
    whole_out = dot_on(attn_cols, late_branch, 1, 0).astype(low).reshape(-1, 2, shard, width)
    out_mine, out_given = by_core(whole_out[:, 0], whole_out[:, 1]), by_core(whole_out[:, 1], whole_out[:, 0])
    whole_out = (wide(out_mine) + wide(mate(out_given))).astype(low).reshape(half_width, width)
    in_parts = sum_parts("parts_in", slots, (whole_in, whole_out), lay_in, in_rows, width)
    grads, in_parts = beside(exchanged_all(grads), in_parts)
    in_parts = sum_corner(in_parts)
    down_parts = sum_xy(down_parts)

    def offset_grads(band, sides, earlier):
        near_sums, far_sums = band_sums_of(after(band, *earlier), sides)
        offset_sums = jnp.dot(near_sums.reshape(-1), place_hot, precision=lax.Precision.HIGHEST)
        far_sums = jnp.sum(far_sums, axis=1)
        end_hot = lax.iota(jnp.int32, 2 * MAXREL + 1)
        offset_sums = offset_sums + jnp.where(end_hot == 0, far_sums[0], 0.0)
        offset_sums = offset_sums + jnp.where(end_hot == 2 * MAXREL, far_sums[1], 0.0)
        return jnp.sum(jnp.where(bucket_hot, offset_sums[:, None], 0.0), axis=0)

    sums, made, sent = (), [], None
    for seq in range(seq_count):
        outs, _, lse = attended[seq]
        done = attend_back(base, edges[seq], far_bias, grads, seq, outs, lse, heads[seq], *bounds[seq], sums)
        if seq == 0:
            done, in_parts, down_parts = beside(done, in_parts, down_parts)
        else:
            done, in_parts, down_sent, made[0] = beside(done, in_parts, down_sent, made[0])
        near_grad, (far_grad,), sums = done
        near_grad = added(near_grad, mate(far_grad), (slice(None), slice(HD, 3 * HD)))
        if seq == 0:
            grads, near_grad = beside(grads, near_grad)
            in_parts = sum_xy(in_parts)
            down_sent = column_sent(down_parts)
        made.append(exchanged(near_grad))
    band, sides = sums
    layer_out = (hidden_one + layer_near + mate(layer_far)).astype(low).reshape(inputs.shape)
    made = [block.reshape(first_cols, 2 * part_len) for block in made]
    first_grads = [dot_on(after(made[0], near_grad), first_w, 0, 1)]
    far_parts = [across_x(first_grads[0][part_len:].astype(low))]
    made[1], rel_grad, far_parts = beside(made[1], offset_grads(band, sides, (near_grad,)), far_parts)
    plan, column = [], 2 * DEPTH * shard
    for k in range(CHIPS):
        z, y, x = turn_of(k)
        plan.append((MATE + k, shard, 0, y * column + (2 * z + x) * shard))
        plan.append((DEVICE + k, shard, 1 + y, (2 * z + x) * shard))
    shapes = ((2 * column, first_cols), (column, first_cols), (column, first_cols))
    given, near, by_y = first_back(slots, tuple(plan), shapes, [block.T for block in first_in], made)
    in_sent = column_sent(after(in_parts, made[1]))
    got = mate(given)
    by_y = across_y((wide(by_y) + wide(got[column:])).astype(low))
    by_y, in_sent = beside(by_y, in_sent)
    first_sent = column_sent((near, got[:column], by_y))
    first_sum = column_total(first_sent)
    first_sums = [first_sum[:shard], across_x(first_sum[shard:])]
    in_sum = column_total(after(in_sent, first_sent[0]))
    grad_down = column_total(down_sent)
    first_grads.append(dot_on(after(made[1], first_sent[0]), first_w, 0, 1))
    far_parts.append(across_x(first_grads[1][part_len:].astype(low)))
    first_grad = all_rows([grad[:part_len] for grad in first_grads]) + wide(all_rows(far_parts))
    input_part = norm_back(first_grad, token_rows, scale_one, gain_one)
    input_grad = (hidden_grad + input_part).astype(low).reshape(inputs.shape)

    grad_query, grad_key, grad_value, norm_sums = by_weight(
        by_side(*first_sums), by_side(*first_sums[::-1]), w_query, w_key, w_value
    )

    hidden_rows = jnp.concatenate([in_sum[:chip_rows], in_sum[chip_rows : 2 * chip_rows]], axis=1)
    mine = by_core(hidden_rows[:shard], hidden_rows[shard:])
    other = mate(by_core(hidden_rows[shard:], hidden_rows[:shard]))
    in_pair = [block.reshape(shard, -1, down_rows) for block in (by_core(mine, other), by_core(other, mine))]
    grad_in = jnp.stack(in_pair, axis=2).reshape(shard, -1)
    grad_out = in_sum[2 * chip_rows :]

    grad_norm_gain = norm_sums[:, 0] / wide(norm_gain)
    grad_ff_gain = jnp.sum(wide(w_in) * grad_in, axis=1) / wide(ff_gain)

    rel_grad = jnp.pad(rel_grad[None, :], ((0, 7), (0, 128 - BUCKETS)))
    rel_sum = (rel_grad + mate(rel_grad))[0]
    rel_mine = by_core(rel_sum[: BUCKETS // 2], rel_sum[BUCKETS // 2 : BUCKETS])

    return (
        in_order(layer_out),
        in_order(input_grad),
        grad_norm_gain,
        grad_query,
        grad_key,
        grad_value,
        grad_out,
        rel_mine,
        grad_ff_gain,
        grad_in,
        grad_down,
    )


def solution(mesh):
    placed = (
        P(None, "blk", "head", None),
        P(),
        P(),
        P(("head", "blk")),
        P(("head", "blk"), None),
        P(("head", "blk"), None),
        P(("head", "blk"), None),
        P(("head", "blk"), None),
        P(("head", "blk")),
        P(("head", "blk")),
        P(("head", "blk"), None),
        P(("head", "blk"), None),
        P(None, "blk", "head", None),
    )
    n_head, n_blk = mesh.shape["head"], mesh.shape["blk"]
    paired = HEADS == 2 * n_head and (n_head, n_blk) == (8, 4)
    return jax.shard_map(
        pair_body if paired else ring_body,
        mesh=mesh,
        in_specs=placed,
        out_specs=(
            P(None, "blk", "head", None),
            P(None, "blk", "head", None),
            P(("head", "blk")),
            P(("head", "blk"), None),
            P(("head", "blk"), None),
            P(("head", "blk"), None),
            P(("head", "blk"), None),
            P(("head", "blk")),
            P(("head", "blk")),
            P(("head", "blk"), None),
            P(("head", "blk"), None),
        ),
        check_vma=False,
    )
```

profile of v0, /device:TPU:0, one launch (start us, length us, event | category | flops | bytes accessed | tf_op | source)
XLA Modules:
  0.0 471.6 jit_solution(7607294182160005177)
XLA Ops:
  13.8 5.1 %collective-permute-start.4 = (bf16[32,1536]{1,0:T(8,128)(2,1)S(1)}, bf16[32,1536]{1,0:T(8,128)(2,1)S(1)}, u32[]{:S(2)}, u32[]{:S(2)}) collective-permute-start(bf16[32,1536]{1,0:T(8,128)(2,1)S(1)} %select_n.164), channel_id=1, source_target_pairs={{0,24},{4,28},{8,16},{12,20},{16,8},{20,12},{24,0},{28,4},{1,25},{... | collective-permute-start | bytes 294920 | tf_op jit(solution)/shard_map/ppermute | solution.py:706
  19.8 1.7 collective-permute-start.1
  25.5 2.3 collective-permute-done.3
  27.8 10.3 %collective-permute-start.9 = (bf16[32,1536]{1,0:T(8,128)(2,1)S(1)}, bf16[32,1536]{1,0:T(8,128)(2,1)}, u32[]{:S(2)}, u32[]{:S(2)}) collective-permute-start(bf16[32,1536]{1,0:T(8,128)(2,1)S(1)} %collective-permute-done.1), channel_id=1, source_target_pairs={{0,24},{4,28},{8,16},{12,20},{16,8},{20,12},{24,0},{28,4},{1,25},{... | collective-permute-start | bytes 294920 | tf_op jit(solution)/shard_map/ppermute | solution.py:706
  40.7 5.2 %all-to-all-start = ((bf16[32,8,128]{2,1,0:T(8,128)(2,1)}), bf16[32,8,128]{2,1,0:T(8,128)(2,1)}, u32[]{:S(2)}, u32[]{:S(2)}) async-start(bf16[32,8,128]{2,1,0:T(8,128)(2,1)} %broadcast_in_dim.81), calls=%async_computation | async-start | bytes 131072 | tf_op jit(solution)/shard_map/all_to_all | solution.py:1193
  46.0 2.4 collective-permute-done.8
  48.4 1.8 pad_maximum_fusion.6
  56.9 2.7 normed_by_seq.1
  59.7 6.4 %collective-permute-done.10 = bf16[128,1536]{1,0:T(8,128)(2,1)} collective-permute-done((bf16[128,1536]{1,0:T(8,128)(2,1)}, bf16[128,1536]{1,0:T(8,128)(2,1)}, u32[]{:S(2)}, u32[]{:S(2)}) %collective-permute-start.10) | collective-permute-done | bytes 393248 | tf_op jit(solution)/shard_map/ppermute | solution.py:706
  67.4 2.0 collective-permute-done.11.arrays_3_
  69.5 2.4 whole_first.1
  71.9 3.9 convolution_convert_fusion.1
  75.7 5.6 %all-to-all-start.1 = ((bf16[8,192,256]{2,1,0:T(8,128)(2,1)}), bf16[8,192,256]{2,1,0:T(8,128)(2,1)S(1)}, u32[]{:S(2)}, u32[]{:S(2)}) async-start(bf16[8,192,256]{2,1,0:T(8,128)(2,1)} %bitcast.7), calls=%async_computation.1 | async-start | bytes 1572864 | tf_op jit(solution)/shard_map/all_to_all | solution.py:1180
  86.4 2.0 copy-done
  88.4 26.3 %all-to-all-done.1.refs_0_ = bf16[8,192,256]{2,1,0:T(8,128)(2,1)S(1)} async-done(((bf16[8,192,256]{2,1,0:T(8,128)(2,1)}), bf16[8,192,256]{2,1,0:T(8,128)(2,1)S(1)}, u32[]{:S(2)}, u32[]{:S(2)}) %all-to-all-start.1) | async-done | bytes 786464 | tf_op jit(solution)/shard_map/all_to_all | solution.py:1180
  114.7 4.2 convolution_convert_fusion
  118.9 3.8 all-to-all-start.2
  123.0 23.9 %attend.2 = (f32[8,64,256]{2,1,0:T(8,128)S(1)}, bf16[16,64,128]{2,1,0:T(8,128)(2,1)}, f32[2,1,2,512]{3,2,1,0:T(2,128)S(1)}) custom-call(s32[5]{0:T(128)S(1)} %pad_add_fusion.2.base_ref, s32[16]{0:T(128)S(1)} %reshape_squeeze.7.edge_ref, f32[2]{0:T(128)S(1)} %pad_maximum_fusion.12.far_ref, bf16[8,192,256]{2,1,0:T(8,128)(2,1)S(1)} %all-to-all-done.1.refs_0_, ...), custom_call_target="tpu_custom_call" | custom-call | flops 1 | bytes 1 | tf_op jit(solution)/shard_map/attend/pallas_call | solution.py:655
  147.7 15.2 %all-to-all-done.2.refs_0_ = bf16[8,192,256]{2,1,0:T(8,128)(2,1)S(1)} async-done(((bf16[8,192,256]{2,1,0:T(8,128)(2,1)}), bf16[8,192,256]{2,1,0:T(8,128)(2,1)S(1)}, u32[]{:S(2)}, u32[]{:S(2)}) %all-to-all-start.2) | async-done | bytes 786464 | tf_op jit(solution)/shard_map/all_to_all | solution.py:1180
  162.9 4.1 all-to-all-start.3
  167.2 12.1 %attend.3 = (f32[8,64,256]{2,1,0:T(8,128)S(1)}, bf16[16,64,128]{2,1,0:T(8,128)(2,1)}, f32[2,1,2,512]{3,2,1,0:T(2,128)S(1)}) custom-call(s32[5]{0:T(128)S(1)} %pad_add_fusion.2.base_ref, s32[16]{0:T(128)S(1)} %reshape_squeeze.6.edge_ref, f32[2]{0:T(128)S(1)} %pad_maximum_fusion.12.far_ref, bf16[8,192,256]{2,1,0:T(8,128)(2,1)S(1)} %all-to-all-done.2.refs_0_, ...), custom_call_target="tpu_custom_call" | custom-call | flops 1 | bytes 1 | tf_op jit(solution)/shard_map/attend/pallas_call | solution.py:655
  180.1 7.0 %all-to-all-start.4 = ((bf16[16,64,128]{2,1,0:T(8,128)(2,1)}), bf16[16,64,128]{2,1,0:T(8,128)(2,1)S(1)}, u32[]{:S(2)}, u32[]{:S(2)}) async-start(bf16[16,64,128]{2,1,0:T(8,128)(2,1)} %get-tuple-element.173), calls=%async_computation.4 | async-start | bytes 524288 | tf_op jit(solution)/shard_map/all_to_all | solution.py:1177
  187.5 8.1 %own_halves.1 = (bf16[1024,2048]{1,0:T(8,128)(2,1)}, bf16[1024,1024]{1,0:T(8,128)(2,1)}, bf16[2048,1024]{1,0:T(8,128)(2,1)}) custom-call(s32[1]{0:T(128)} %bitcast.16.place_ref, bf16[32,288,1024]{2,1,0:T(8,128)(2,1)} %bitcast.106, bf16[32,288,1024]{2,1,0:T(8,128)(2,1)} %bitcast.107, bf16[32,288,1024]{2,1,0:T(8,128)(2,1)} %bitcast.108, ...), custom_call_target="tpu_custom_call" | custom-call | tf_op jit(solution)/shard_map/own_halves/pallas_call | solution.py:1041
  197.2 2.6 multiply_reduce_fusion.2
  200.7 1.7 pad_maximum_fusion.1.grad_ref.right_ref
  202.6 14.2 %feed.1 = (bf16[512,2048]{1,0:T(8,128)(2,1)}, bf16[512,2048]{1,0:T(8,128)(2,1)}, f32[256,1024]{1,0:T(8,128)}, f32[256,1024]{1,0:T(8,128)}, f32[256,1024]{1,0:T(8,128)}, /*index=5*/f32[256,1024]{1,0:T(8,128)}) custom-call(bf16[512,1024]{1,0:T(8,128)(2,1)S(1)} %pad_maximum_fusion.rows_ref.left_ref, bf16[512,1024]{1,0:T(8,128)(2,1)S(1)} %pad_maximum_fusion.1.grad_ref.right_ref, ...), custom_call_target="tpu_custom_call" | custom-call | flops 1 | bytes 1 | tf_op jit(solution)/shard_map/feed/pallas_call | solution.py:929
  217.4 4.7 %weight_grad.2.arrays_0_ = bf16[2048,1024]{1,0:T(8,128)(2,1)S(1)} custom-call(bf16[512,2048]{1,0:T(8,128)(2,1)} %get-tuple-element.186.left_ref, bf16[512,1024]{1,0:T(8,128)(2,1)} %copy-done.2), custom_call_target="tpu_custom_call" | custom-call | flops 1 | bytes 1 | tf_op jit(solution)/shard_map/weight_grad/pallas_call | solution.py:955
  222.2 2.8 parts_down.1
  227.4 3.1 fusion.21
  232.1 7.0 %collective-permute-done.18.part_ref = bf16[256,1024]{1,0:T(8,128)(2,1)S(1)} collective-permute-done((bf16[256,1024]{1,0:T(8,128)(2,1)}, bf16[256,1024]{1,0:T(8,128)(2,1)S(1)}, u32[]{:S(2)}, u32[]{:S(2)}) %collective-permute-start.18) | collective-permute-done | bytes 524320 | tf_op jit(solution)/shard_map/ppermute | solution.py:706
  242.9 6.0 %all-to-all-start.5 = ((bf16[16,64,256]{2,1,0:T(8,128)(2,1)}), bf16[16,64,256]{2,1,0:T(8,128)(2,1)}, u32[]{:S(2)}, u32[]{:S(2)}) async-start(bf16[16,64,256]{2,1,0:T(8,128)(2,1)} %bitcast.128), calls=%async_computation.5 | async-start | bytes 1048576 | tf_op jit(solution)/shard_map/all_to_all | solution.py:1177
  250.1 2.0 collective-permute-start.23
  254.7 4.5 weight_grad.3.arrays_0_
  259.2 1.9 fusion.2
  261.1 3.2 parts_in.1
  266.2 35.5 %attend_back.2 = (bf16[8,192,256]{2,1,0:T(8,128)(2,1)}, bf16[8,128,256]{2,1,0:T(8,128)(2,1)}, f32[2048,512]{1,0:T(8,128)}, f32[8,512]{1,0:T(8,128)}) custom-call(s32[5]{0:T(128)} %copy-done.33, s32[16]{0:T(128)} %copy-done.35, f32[2]{0:T(128)} %copy-done.30, bf16[16,64,256]{2,1,0:T(8,128)(2,1)} %all-to-all-done.5.g_ref, f32[8,64,256]{2,1,0:T(8,128)} %copy-done.24, ...), custom_call_target="tpu_custom_call" | custom-call | flops 1 | bytes 1 | tf_op jit(solution)/shard_map/attend_back/pallas_call | solution.py:681
  303.5 2.1 collective-permute-done.25.part_ref
  307.8 5.1 %all-to-all-start.6 = ((bf16[8,192,256]{2,1,0:T(8,128)(2,1)}), bf16[8,192,256]{2,1,0:T(8,128)(2,1)}, u32[]{:S(2)}, u32[]{:S(2)}) async-start(bf16[8,192,256]{2,1,0:T(8,128)(2,1)} %added.8), calls=%async_computation.6 | async-start | bytes 1572864 | tf_op jit(solution)/shard_map/all_to_all | solution.py:1180
  314.2 2.1 collective-permute-start.27
  318.0 1.6 column.3
  321.2 2.4 collective-permute-start.29
  324.1 21.0 %attend_back.3 = (bf16[8,192,256]{2,1,0:T(8,128)(2,1)}, bf16[8,128,256]{2,1,0:T(8,128)(2,1)}, f32[2048,512]{1,0:T(8,128)}, f32[8,512]{1,0:T(8,128)}) custom-call(s32[5]{0:T(128)} %copy-done.33, s32[16]{0:T(128)} %copy-done.34, f32[2]{0:T(128)} %copy-done.30, bf16[16,64,256]{2,1,0:T(8,128)(2,1)} %all-to-all-done.5.g_ref, f32[8,64,256]{2,1,0:T(8,128)} %copy-done.23, ...), custom_call_target="tpu_custom_call" | custom-call | flops 1 | bytes 1 | tf_op jit(solution)/shard_map/attend_back/pallas_call | solution.py:681
  345.2 6.1 %collective-permute-done.29 = bf16[128,1024]{1,0:T(8,128)(2,1)S(1)} collective-permute-done((bf16[128,1024]{1,0:T(8,128)(2,1)S(1)}, bf16[128,1024]{1,0:T(8,128)(2,1)S(1)}, u32[]{:S(2)}, u32[]{:S(2)}) %collective-permute-start.29) | collective-permute-done | bytes 262176 | tf_op jit(solution)/shard_map/ppermute | solution.py:706
  352.1 2.1 collective-permute-done.31.part_ref
  356.4 7.3 %all-to-all-start.7 = ((bf16[8,192,256]{2,1,0:T(8,128)(2,1)}), bf16[8,192,256]{2,1,0:T(8,128)(2,1)}, u32[]{:S(2)}, u32[]{:S(2)}) async-start(bf16[8,192,256]{2,1,0:T(8,128)(2,1)} %added.11), calls=%async_computation.7 | async-start | bytes 1572864 | tf_op jit(solution)/shard_map/all_to_all | solution.py:1180
  363.7 2.0 copy.129
  365.8 2.0 copy.130
  367.8 3.3 fusion.36
  373.7 2.4 band_sums.1
  376.9 2.0 fusion.5
  380.6 3.4 all-to-all-done.7
  384.0 5.3 %first_back.1 = (bf16[512,1536]{1,0:T(8,128)(2,1)}, bf16[256,1536]{1,0:T(8,128)(2,1)}, bf16[256,1536]{1,0:T(8,128)(2,1)}) custom-call(s32[64]{0:T(128)S(1)} %pad_add_fusion.3.slots_ref, bf16[1024,256]{1,0:T(8,128)(2,1)} %bitcast.122, bf16[1536,256]{1,0:T(8,128)(2,1)} %bitcast.31.made_0, bf16[1024,256]{1,0:T(8,128)(2,1)} %bitcast.123, ...), custom_call_target="tpu_custom_call" | custom-call | tf_op jit(solution)/shard_map/first_back/pallas_call | solution.py:984
  390.5 2.5 collective-permute-done.33
  393.0 1.6 add_convert_fusion
  398.7 2.0 collective-permute-start.36
  400.7 2.4 collective-permute-start.37
  404.8 9.8 %collective-permute-done.35 = bf16[160,1024]{1,0:T(8,128)(2,1)S(1)} collective-permute-done((bf16[160,1024]{1,0:T(8,128)(2,1)S(1)}, bf16[160,1024]{1,0:T(8,128)(2,1)S(1)}, u32[]{:S(2)}, u32[]{:S(2)}) %collective-permute-start.35) | collective-permute-done | bytes 327712 | tf_op jit(solution)/shard_map/ppermute | solution.py:706
  414.6 9.6 %collective-permute-done.36 = bf16[160,1024]{1,0:T(8,128)(2,1)S(1)} collective-permute-done((bf16[160,1024]{1,0:T(8,128)(2,1)S(1)}, bf16[160,1024]{1,0:T(8,128)(2,1)S(1)}, u32[]{:S(2)}, u32[]{:S(2)}) %collective-permute-start.36) | collective-permute-done | bytes 327712 | tf_op jit(solution)/shard_map/ppermute | solution.py:706
  426.5 2.2 fusion.37
  428.7 7.2 %collective-permute-start.39 = (bf16[64,1536]{1,0:T(8,128)(2,1)S(1)}, bf16[64,1536]{1,0:T(8,128)(2,1)S(1)}, u32[]{:S(2)}, u32[]{:S(2)}) collective-permute-start(bf16[64,1536]{1,0:T(8,128)(2,1)S(1)} %get-tuple-element.263), channel_id=1, source_target_pairs={{0,8},{4,12},{8,0},{12,4},{16,24},{20,28},{24,16},{28,20},{1,9},{5... | collective-permute-start | bytes 589832 | tf_op jit(solution)/shard_map/ppermute | solution.py:706
  436.0 2.4 collective-permute-start.41
  440.0 3.6 collective-permute-done.39
  443.6 9.5 %collective-permute-done.40 = bf16[64,1536]{1,0:T(8,128)(2,1)S(1)} collective-permute-done((bf16[64,1536]{1,0:T(8,128)(2,1)S(1)}, bf16[64,1536]{1,0:T(8,128)(2,1)S(1)}, u32[]{:S(2)}, u32[]{:S(2)}) %collective-permute-start.40) | collective-permute-done | bytes 196640 | tf_op jit(solution)/shard_map/ppermute | solution.py:706
  460.9 2.0 by_weight.1
  (372 shorter events, 81.5 us)
Async XLA Ops:
  7.2 180.3 %all-gather.3.cloned.1.call-start = ((), (), s32[]{:S(2)}) async-start(), calls=%async_computation.8 | async-start | bytes 19464192 | tf_op jit(solution)/shard_map/all_gather | solution.py:1225
  13.8 11.7 %collective-permute-start.4 = (bf16[32,1536]{1,0:T(8,128)(2,1)S(1)}, bf16[32,1536]{1,0:T(8,128)(2,1)S(1)}, u32[]{:S(2)}, u32[]{:S(2)}) collective-permute-start(bf16[32,1536]{1,0:T(8,128)(2,1)S(1)} %select_n.164), channel_id=1, source_target_pairs={{0,24},{4,28},{8,16},{12,20},{16,8},{20,12},{24,0},{28,4},{1,25},{... | collective-permute-start | bytes 294920 | tf_op jit(solution)/shard_map/ppermute | solution.py:706
  18.9 8.8 %collective-permute-start.3 = (bf16[32,1536]{1,0:T(8,128)(2,1)S(1)}, bf16[32,1536]{1,0:T(8,128)(2,1)S(1)}, u32[]{:S(2)}, u32[]{:S(2)}) collective-permute-start(bf16[32,1536]{1,0:T(8,128)(2,1)S(1)} %select_n.164), channel_id=1, source_target_pairs={{0,16},{4,20},{8,24},{12,28},{16,0},{20,4},{24,8},{28,12},{1,17},{... | collective-permute-start | bytes 294920 | tf_op jit(solution)/shard_map/ppermute | solution.py:706
  18.9 8.8 %collective-permute-start.2 = (bf16[32,1536]{1,0:T(8,128)(2,1)S(1)}, bf16[32,1536]{1,0:T(8,128)(2,1)S(1)}, u32[]{:S(2)}, u32[]{:S(2)}) collective-permute-start(bf16[32,1536]{1,0:T(8,128)(2,1)S(1)} %select_n.164), channel_id=1, source_target_pairs={{0,8},{4,12},{8,0},{12,4},{16,24},{20,28},{24,16},{28,20},{1,9},{5... | collective-permute-start | bytes 294920 | tf_op jit(solution)/shard_map/ppermute | solution.py:706
  19.8 8.0 %collective-permute-start.1 = (bf16[32,1536]{1,0:T(8,128)(2,1)S(1)}, bf16[32,1536]{1,0:T(8,128)(2,1)S(1)}, u32[]{:S(2)}, u32[]{:S(2)}) collective-permute-start(bf16[32,1536]{1,0:T(8,128)(2,1)S(1)} %select_n.161), channel_id=1, source_target_pairs={{0,2},{1,3},{2,0},{3,1},{4,6},{5,7},{6,4},{7,5},{8,10},{9,11},{10,... | collective-permute-start | bytes 294920 | tf_op jit(solution)/shard_map/ppermute | solution.py:706
  23.5 32.5 %copy-start.53 = (bf16[2,128,1024]{2,1,0:T(8,128)(2,1)}, bf16[2,128,1024]{2,1,0:T(8,128)(2,1)S(1)}, u32[]{:S(2)}) copy-start(bf16[2,128,1024]{2,1,0:T(8,128)(2,1)S(1)} %fusion.7.here_ref) | copy-start | bytes 1572868
  23.6 32.6 %collective-permute-start = (bf16[2,128,1024]{2,1,0:T(8,128)(2,1)S(1)}, bf16[2,128,1024]{2,1,0:T(8,128)(2,1)S(1)}, u32[]{:S(2)}, u32[]{:S(2)}) collective-permute-start(bf16[2,128,1024]{2,1,0:T(8,128)(2,1)S(1)} %fusion.7.here_ref), channel_id=1, source_target_pairs={{0,2},{1,3},{2,0},{3,1},{4,6},{5,7},{6,4},{7,5},{8,10},{9,11},{10,... | collective-permute-start | bytes 1572872 | tf_op jit(solution)/shard_map/ppermute | solution.py:706
  27.8 18.2 %collective-permute-start.9 = (bf16[32,1536]{1,0:T(8,128)(2,1)S(1)}, bf16[32,1536]{1,0:T(8,128)(2,1)}, u32[]{:S(2)}, u32[]{:S(2)}) collective-permute-start(bf16[32,1536]{1,0:T(8,128)(2,1)S(1)} %collective-permute-done.1), channel_id=1, source_target_pairs={{0,24},{4,28},{8,16},{12,20},{16,8},{20,12},{24,0},{28,4},{1,25},{... | collective-permute-start | bytes 294920 | tf_op jit(solution)/shard_map/ppermute | solution.py:706
  38.0 10.3 %collective-permute-start.8 = (bf16[32,1536]{1,0:T(8,128)(2,1)S(1)}, bf16[32,1536]{1,0:T(8,128)(2,1)}, u32[]{:S(2)}, u32[]{:S(2)}) collective-permute-start(bf16[32,1536]{1,0:T(8,128)(2,1)S(1)} %collective-permute-done.1), channel_id=1, source_target_pairs={{0,16},{4,20},{8,24},{12,28},{16,0},{20,4},{24,8},{28,12},{1,17},{... | collective-permute-start | bytes 294920 | tf_op jit(solution)/shard_map/ppermute | solution.py:706
  38.0 10.3 %collective-permute-start.7 = (bf16[32,1536]{1,0:T(8,128)(2,1)S(1)}, bf16[32,1536]{1,0:T(8,128)(2,1)}, u32[]{:S(2)}, u32[]{:S(2)}) collective-permute-start(bf16[32,1536]{1,0:T(8,128)(2,1)S(1)} %collective-permute-done.1), channel_id=1, source_target_pairs={{0,8},{4,12},{8,0},{12,4},{16,24},{20,28},{24,16},{28,20},{1,9},{5... | collective-permute-start | bytes 294920 | tf_op jit(solution)/shard_map/ppermute | solution.py:706
  38.7 17.3 %collective-permute-start.5 = (bf16[128,1536]{1,0:T(8,128)(2,1)S(1)}, bf16[128,1536]{1,0:T(8,128)(2,1)S(1)}, u32[]{:S(2)}, u32[]{:S(2)}) collective-permute-start(bf16[128,1536]{1,0:T(8,128)(2,1)S(1)} %pad_maximum_fusion.5), channel_id=1, source_target_pairs={{0,4},{4,0},{8,12},{12,8},{16,20},{20,16},{24,28},{28,24},{1,5},{5... | collective-permute-start | bytes 1179656 | tf_op jit(solution)/shard_map/ppermute | solution.py:706
  40.7 13.7 %all-to-all-start = ((bf16[32,8,128]{2,1,0:T(8,128)(2,1)}), bf16[32,8,128]{2,1,0:T(8,128)(2,1)}, u32[]{:S(2)}, u32[]{:S(2)}) async-start(bf16[32,8,128]{2,1,0:T(8,128)(2,1)} %broadcast_in_dim.81), calls=%async_computation | async-start | bytes 131072 | tf_op jit(solution)/shard_map/all_to_all | solution.py:1193
  50.1 15.9 %collective-permute-start.10 = (bf16[128,1536]{1,0:T(8,128)(2,1)}, bf16[128,1536]{1,0:T(8,128)(2,1)}, u32[]{:S(2)}, u32[]{:S(2)}) collective-permute-start(bf16[128,1536]{1,0:T(8,128)(2,1)} %pad_maximum_fusion.6), channel_id=1, source_target_pairs={{0,4},{4,0},{8,12},{12,8},{16,20},{20,16},{24,28},{28,24},{1,5},{5... | collective-permute-start | bytes 1179656 | tf_op jit(solution)/shard_map/ppermute | solution.py:706
  56.1 11.4 %collective-permute-start.6 = (bf16[256,1536]{1,0:T(8,128)(2,1)S(1)}, bf16[256,1536]{1,0:T(8,128)(2,1)S(1)}, u32[]{:S(2)}, u32[]{:S(2)}) collective-permute-start(bf16[256,1536]{1,0:T(8,128)(2,1)S(1)} %constant_dynamic-update-slice_fusion.arrays_0_), channel_id=1, source_target_pairs={{0,1},{1,0},{2,3},{3,2},{4,5},{5,4},{6,7},{7,6},{8,9},{9,8},{10,11... | collective-permute-start | bytes 2359304 | tf_op jit(solution)/shard_map/ppermute | solution.py:706
  67.1 2.4 collective-permute-start.11
  75.7 38.9 %all-to-all-start.1 = ((bf16[8,192,256]{2,1,0:T(8,128)(2,1)}), bf16[8,192,256]{2,1,0:T(8,128)(2,1)S(1)}, u32[]{:S(2)}, u32[]{:S(2)}) async-start(bf16[8,192,256]{2,1,0:T(8,128)(2,1)} %bitcast.7), calls=%async_computation.1 | async-start | bytes 1572864 | tf_op jit(solution)/shard_map/all_to_all | solution.py:1180
  85.2 81.9 %copy-start.30 = (f32[2]{0:T(128)}, f32[2]{0:T(128)S(1)}, u32[]{:S(2)}) copy-start(f32[2]{0:T(128)S(1)} %pad_maximum_fusion.12.far_ref) | copy-start | bytes 28
  85.2 29.5 %copy-start.59 = (bf16[256,1024]{1,0:T(8,128)(2,1)S(1)}, bf16[256,1024]{1,0:T(8,128)(2,1)}, u32[]{:S(2)}) copy-start(bf16[256,1024]{1,0:T(8,128)(2,1)} %get-tuple-element.158) | copy-start | bytes 1572868
  88.4 34.3 %copy-start.85 = (s32[4]{0:T(128)S(1)}, s32[4]{0:T(128)}, u32[]{:S(2)}) copy-start(s32[4]{0:T(128)} %constant.87.clone) | copy-start | bytes 52
  114.7 4.2 collective-permute-start.12
  118.9 27.9 %copy-start.9 = (bf16[8,192,256]{2,1,0:T(8,128)(2,1)}, bf16[8,192,256]{2,1,0:T(8,128)(2,1)S(1)}, u32[]{:S(2)}) copy-start(bf16[8,192,256]{2,1,0:T(8,128)(2,1)S(1)} %collective-permute-done.12.refs_1_) | copy-start | bytes 2359300
  118.9 43.9 %all-to-all-start.2 = ((bf16[8,192,256]{2,1,0:T(8,128)(2,1)}), bf16[8,192,256]{2,1,0:T(8,128)(2,1)S(1)}, u32[]{:S(2)}, u32[]{:S(2)}) async-start(bf16[8,192,256]{2,1,0:T(8,128)(2,1)} %bitcast.127), calls=%async_computation.2 | async-start | bytes 1572864 | tf_op jit(solution)/shard_map/all_to_all | solution.py:1180
  122.8 44.3 %copy-start.33 = (s32[5]{0:T(128)}, s32[5]{0:T(128)S(1)}, u32[]{:S(2)}) copy-start(s32[5]{0:T(128)S(1)} %pad_add_fusion.2.base_ref) | copy-start | bytes 64
  122.9 44.2 %copy-start.25 = (s32[2,1,2,512]{3,2,1,0:T(2,128)}, s32[2,1,2,512]{3,2,1,0:T(2,128)S(1)}, u32[]{:S(2)}) copy-start(s32[2,1,2,512]{3,2,1,0:T(2,128)S(1)} %get-tuple-element.395.refs_2_) | copy-start | bytes 24580
  123.0 44.2 %copy-start.26 = (s32[2,1,2,512]{3,2,1,0:T(2,128)}, s32[2,1,2,512]{3,2,1,0:T(2,128)S(1)}, u32[]{:S(2)}) copy-start(s32[2,1,2,512]{3,2,1,0:T(2,128)S(1)} %get-tuple-element.393.refs_3_) | copy-start | bytes 24580
  147.7 31.6 %copy-start.32 = (f32[2,1,2,512]{3,2,1,0:T(2,128)}, f32[2,1,2,512]{3,2,1,0:T(2,128)S(1)}, u32[]{:S(2)}) copy-start(f32[2,1,2,512]{3,2,1,0:T(2,128)S(1)} %get-tuple-element.202.lse_ref) | copy-start | bytes 24580
  162.9 4.2 collective-permute-start.13
  162.9 17.3 %all-to-all-start.3 = ((bf16[16,64,128]{2,1,0:T(8,128)(2,1)}), bf16[16,64,128]{2,1,0:T(8,128)(2,1)S(1)}, u32[]{:S(2)}, u32[]{:S(2)}) async-start(bf16[16,64,128]{2,1,0:T(8,128)(2,1)} %get-tuple-element.171), calls=%async_computation.3 | async-start | bytes 524288 | tf_op jit(solution)/shard_map/all_to_all | solution.py:1177
  180.1 17.0 %all-to-all-start.4 = ((bf16[16,64,128]{2,1,0:T(8,128)(2,1)}), bf16[16,64,128]{2,1,0:T(8,128)(2,1)S(1)}, u32[]{:S(2)}, u32[]{:S(2)}) async-start(bf16[16,64,128]{2,1,0:T(8,128)(2,1)} %get-tuple-element.173), calls=%async_computation.4 | async-start | bytes 524288 | tf_op jit(solution)/shard_map/all_to_all | solution.py:1177
  187.3 13.4 %collective-permute-start.15 = (bf16[256,1024]{1,0:T(8,128)(2,1)S(1)}, bf16[256,1024]{1,0:T(8,128)(2,1)}, u32[]{:S(2)}, u32[]{:S(2)}) collective-permute-start(bf16[256,1024]{1,0:T(8,128)(2,1)S(1)} %bitcast.114), channel_id=1, source_target_pairs={{0,1},{1,0},{2,3},{3,2},{4,5},{5,4},{6,7},{7,6},{8,9},{9,8},{10,11... | collective-permute-start | bytes 1572872 | tf_op jit(solution)/shard_map/ppermute | solution.py:706
  200.0 2.5 collective-permute-start.14
  216.9 10.2 %collective-permute-start.17 = (f32[256,1024]{1,0:T(8,128)}, f32[256,1024]{1,0:T(8,128)S(1)}, u32[]{:S(2)}, u32[]{:S(2)}) collective-permute-start(f32[256,1024]{1,0:T(8,128)} %get-tuple-element.184), channel_id=1, source_target_pairs={{0,1},{1,0},{2,3},{3,2},{4,5},{5,4},{6,7},{7,6},{8,9},{9,8},{10,11... | collective-permute-start | bytes 3145736 | tf_op jit(solution)/shard_map/ppermute | solution.py:706
  216.9 10.4 %collective-permute-start.16 = (f32[256,1024]{1,0:T(8,128)}, f32[256,1024]{1,0:T(8,128)}, u32[]{:S(2)}, u32[]{:S(2)}) collective-permute-start(f32[256,1024]{1,0:T(8,128)} %get-tuple-element.182), channel_id=1, source_target_pairs={{0,1},{1,0},{2,3},{3,2},{4,5},{5,4},{6,7},{7,6},{8,9},{9,8},{10,11... | collective-permute-start | bytes 3145736 | tf_op jit(solution)/shard_map/ppermute | solution.py:706
  225.0 14.1 %collective-permute-start.18 = (bf16[256,1024]{1,0:T(8,128)(2,1)}, bf16[256,1024]{1,0:T(8,128)(2,1)S(1)}, u32[]{:S(2)}, u32[]{:S(2)}) collective-permute-start(bf16[256,1024]{1,0:T(8,128)(2,1)} %get-tuple-element.190), channel_id=1, source_target_pairs={{0,4},{4,0},{8,12},{12,8},{16,20},{20,16},{24,28},{28,24},{1,5},{5... | collective-permute-start | bytes 1572872 | tf_op jit(solution)/shard_map/ppermute | solution.py:706
  225.9 13.8 %collective-permute-start.19 = (bf16[256,1024]{1,0:T(8,128)(2,1)}, bf16[256,1024]{1,0:T(8,128)(2,1)S(1)}, u32[]{:S(2)}, u32[]{:S(2)}) collective-permute-start(bf16[256,1024]{1,0:T(8,128)(2,1)} %get-tuple-element.191), channel_id=1, source_target_pairs={{0,2},{1,3},{2,0},{3,1},{4,6},{5,7},{6,4},{7,5},{8,10},{9,11},{10,... | collective-permute-start | bytes 1572872 | tf_op jit(solution)/shard_map/ppermute | solution.py:706
  242.9 16.3 %collective-permute-start.20 = (bf16[16,32,1024]{2,1,0:T(8,128)(2,1)}, bf16[16,32,1024]{2,1,0:T(8,128)(2,1)}, u32[]{:S(2)}, u32[]{:S(2)}) collective-permute-start(bf16[16,32,1024]{2,1,0:T(8,128)(2,1)} %select_bitcast_fusion), channel_id=1, source_target_pairs={{0,1},{1,0},{2,3},{3,2},{4,5},{5,4},{6,7},{7,6},{8,9},{9,8},{10,11... | collective-permute-start | bytes 3145736 | tf_op jit(solution)/shard_map/ppermute | solution.py:706
  242.9 21.5 %all-to-all-start.5 = ((bf16[16,64,256]{2,1,0:T(8,128)(2,1)}), bf16[16,64,256]{2,1,0:T(8,128)(2,1)}, u32[]{:S(2)}, u32[]{:S(2)}) async-start(bf16[16,64,256]{2,1,0:T(8,128)(2,1)} %bitcast.128), calls=%async_computation.5 | async-start | bytes 1048576 | tf_op jit(solution)/shard_map/all_to_all | solution.py:1177
  250.1 51.6 %collective-permute-start.23 = (bf16[512,1024]{1,0:T(8,128)(2,1)}, bf16[512,1024]{1,0:T(8,128)(2,1)S(1)}, u32[]{:S(2)}, u32[]{:S(2)}) collective-permute-start(bf16[512,1024]{1,0:T(8,128)(2,1)} %added.6), channel_id=1, source_target_pairs={{0,2},{1,3},{2,0},{3,1},{4,6},{5,7},{6,4},{7,5},{8,10},{9,11},{10,... | collective-permute-start | bytes 3145736 | tf_op jit(solution)/shard_map/ppermute | solution.py:706
  253.2 49.4 %collective-permute-start.24 = (bf16[512,1024]{1,0:T(8,128)(2,1)}, bf16[512,1024]{1,0:T(8,128)(2,1)}, u32[]{:S(2)}, u32[]{:S(2)}) collective-permute-start(bf16[512,1024]{1,0:T(8,128)(2,1)} %added.7), channel_id=1, source_target_pairs={{0,4},{4,0},{8,12},{12,8},{16,20},{20,16},{24,28},{28,24},{1,5},{5... | collective-permute-start | bytes 3145736 | tf_op jit(solution)/shard_map/ppermute | solution.py:706
  264.4 38.3 %collective-permute-start.21 = (bf16[320,1024]{1,0:T(8,128)(2,1)}, bf16[320,1024]{1,0:T(8,128)(2,1)S(1)}, u32[]{:S(2)}, u32[]{:S(2)}) collective-permute-start(bf16[320,1024]{1,0:T(8,128)(2,1)} %get-tuple-element.210), channel_id=1, source_target_pairs={{0,4},{4,0},{8,12},{12,8},{16,20},{20,16},{24,28},{28,24},{1,5},{5... | collective-permute-start | bytes 1966088 | tf_op jit(solution)/shard_map/ppermute | solution.py:706
  265.6 37.1 %collective-permute-start.22 = (bf16[320,1024]{1,0:T(8,128)(2,1)}, bf16[320,1024]{1,0:T(8,128)(2,1)S(1)}, u32[]{:S(2)}, u32[]{:S(2)}) collective-permute-start(bf16[320,1024]{1,0:T(8,128)(2,1)} %get-tuple-element.211), channel_id=1, source_target_pairs={{0,2},{1,3},{2,0},{3,1},{4,6},{5,7},{6,4},{7,5},{8,10},{9,11},{10,... | collective-permute-start | bytes 1966088 | tf_op jit(solution)/shard_map/ppermute | solution.py:706
  303.5 2.1 collective-permute-start.25
  307.8 44.3 %all-to-all-start.6 = ((bf16[8,192,256]{2,1,0:T(8,128)(2,1)}), bf16[8,192,256]{2,1,0:T(8,128)(2,1)}, u32[]{:S(2)}, u32[]{:S(2)}) async-start(bf16[8,192,256]{2,1,0:T(8,128)(2,1)} %added.8), calls=%async_computation.6 | async-start | bytes 1572864 | tf_op jit(solution)/shard_map/all_to_all | solution.py:1180
  314.2 37.8 %collective-permute-start.27 = (bf16[640,1024]{1,0:T(8,128)(2,1)S(1)}, bf16[640,1024]{1,0:T(8,128)(2,1)S(1)}, u32[]{:S(2)}, u32[]{:S(2)}) collective-permute-start(bf16[640,1024]{1,0:T(8,128)(2,1)S(1)} %added.10), channel_id=1, source_target_pairs={{0,4},{4,0},{8,12},{12,8},{16,20},{20,16},{24,28},{28,24},{1,5},{5... | collective-permute-start | bytes 3932168 | tf_op jit(solution)/shard_map/ppermute | solution.py:706
  316.5 35.6 %collective-permute-start.26 = (bf16[640,1024]{1,0:T(8,128)(2,1)S(1)}, bf16[640,1024]{1,0:T(8,128)(2,1)S(1)}, u32[]{:S(2)}, u32[]{:S(2)}) collective-permute-start(bf16[640,1024]{1,0:T(8,128)(2,1)S(1)} %added.9), channel_id=1, source_target_pairs={{0,2},{1,3},{2,0},{3,1},{4,6},{5,7},{6,4},{7,5},{8,10},{9,11},{10,... | collective-permute-start | bytes 3932168 | tf_op jit(solution)/shard_map/ppermute | solution.py:706
  319.6 25.5 %collective-permute-start.28 = (bf16[128,1024]{1,0:T(8,128)(2,1)S(1)}, bf16[128,1024]{1,0:T(8,128)(2,1)S(1)}, u32[]{:S(2)}, u32[]{:S(2)}) collective-permute-start(bf16[128,1024]{1,0:T(8,128)(2,1)S(1)} %get-tuple-element.232), channel_id=1, source_target_pairs={{0,8},{4,12},{8,0},{12,4},{16,24},{20,28},{24,16},{28,20},{1,9},{5... | collective-permute-start | bytes 786440 | tf_op jit(solution)/shard_map/ppermute | solution.py:706
  321.2 30.0 %collective-permute-start.29 = (bf16[128,1024]{1,0:T(8,128)(2,1)S(1)}, bf16[128,1024]{1,0:T(8,128)(2,1)S(1)}, u32[]{:S(2)}, u32[]{:S(2)}) collective-permute-start(bf16[128,1024]{1,0:T(8,128)(2,1)S(1)} %get-tuple-element.233), channel_id=1, source_target_pairs={{0,16},{4,20},{8,24},{12,28},{16,0},{20,4},{24,8},{28,12},{1,17},{... | collective-permute-start | bytes 786440 | tf_op jit(solution)/shard_map/ppermute | solution.py:706
  323.5 27.7 %collective-permute-start.30 = (bf16[128,1024]{1,0:T(8,128)(2,1)S(1)}, bf16[128,1024]{1,0:T(8,128)(2,1)S(1)}, u32[]{:S(2)}, u32[]{:S(2)}) collective-permute-start(bf16[128,1024]{1,0:T(8,128)(2,1)S(1)} %get-tuple-element.234), channel_id=1, source_target_pairs={{0,24},{4,28},{8,16},{12,20},{16,8},{20,12},{24,0},{28,4},{1,25},{... | collective-permute-start | bytes 786440 | tf_op jit(solution)/shard_map/ppermute | solution.py:706
  352.1 2.2 collective-permute-start.31
  356.4 27.6 %all-to-all-start.7 = ((bf16[8,192,256]{2,1,0:T(8,128)(2,1)}), bf16[8,192,256]{2,1,0:T(8,128)(2,1)}, u32[]{:S(2)}, u32[]{:S(2)}) async-start(bf16[8,192,256]{2,1,0:T(8,128)(2,1)} %added.11), calls=%async_computation.7 | async-start | bytes 1572864 | tf_op jit(solution)/shard_map/all_to_all | solution.py:1180
  372.2 8.4 %collective-permute-start.32 = (bf16[128,1024]{1,0:T(8,128)(2,1)}, bf16[128,1024]{1,0:T(8,128)(2,1)}, u32[]{:S(2)}, u32[]{:S(2)}) collective-permute-start(bf16[128,1024]{1,0:T(8,128)(2,1)} %slice.275), channel_id=1, source_target_pairs={{0,2},{1,3},{2,0},{3,1},{4,6},{5,7},{6,4},{7,5},{8,10},{9,11},{10,... | collective-permute-start | bytes 786440 | tf_op jit(solution)/shard_map/ppermute | solution.py:706
  389.3 3.8 collective-permute-start.33
  394.7 29.6 %collective-permute-start.34 = (bf16[256,1536]{1,0:T(8,128)(2,1)S(1)}, bf16[256,1536]{1,0:T(8,128)(2,1)S(1)}, u32[]{:S(2)}, u32[]{:S(2)}) collective-permute-start(bf16[256,1536]{1,0:T(8,128)(2,1)S(1)} %add_convert_fusion), channel_id=1, source_target_pairs={{0,4},{4,0},{8,12},{12,8},{16,20},{20,16},{24,28},{28,24},{1,5},{5... | collective-permute-start | bytes 2359304 | tf_op jit(solution)/shard_map/ppermute | solution.py:706
  397.1 6.0 %collective-permute-start.43 = (f32[8,128]{1,0:T(8,128)S(1)}, f32[8,128]{1,0:T(8,128)S(1)}, u32[]{:S(2)}, u32[]{:S(2)}) collective-permute-start(f32[8,128]{1,0:T(8,128)S(1)} %pad.9), channel_id=1, source_target_pairs={{0,1},{1,0},{2,3},{3,2},{4,5},{5,4},{6,7},{7,6},{8,9},{9,8},{10,11... | collective-permute-start | bytes 12296 | tf_op jit(solution)/shard_map/ppermute | solution.py:706
  398.6 16.0 %collective-permute-start.35 = (bf16[160,1024]{1,0:T(8,128)(2,1)S(1)}, bf16[160,1024]{1,0:T(8,128)(2,1)S(1)}, u32[]{:S(2)}, u32[]{:S(2)}) collective-permute-start(bf16[160,1024]{1,0:T(8,128)(2,1)S(1)} %get-tuple-element.256), channel_id=1, source_target_pairs={{0,8},{4,12},{8,0},{12,4},{16,24},{20,28},{24,16},{28,20},{1,9},{5... | collective-permute-start | bytes 983048 | tf_op jit(solution)/shard_map/ppermute | solution.py:706
  398.7 25.6 %collective-permute-start.36 = (bf16[160,1024]{1,0:T(8,128)(2,1)S(1)}, bf16[160,1024]{1,0:T(8,128)(2,1)S(1)}, u32[]{:S(2)}, u32[]{:S(2)}) collective-permute-start(bf16[160,1024]{1,0:T(8,128)(2,1)S(1)} %get-tuple-element.257), channel_id=1, source_target_pairs={{0,16},{4,20},{8,24},{12,28},{16,0},{20,4},{24,8},{28,12},{1,17},{... | collective-permute-start | bytes 983048 | tf_op jit(solution)/shard_map/ppermute | solution.py:706
  400.7 23.6 %collective-permute-start.37 = (bf16[160,1024]{1,0:T(8,128)(2,1)S(1)}, bf16[160,1024]{1,0:T(8,128)(2,1)S(1)}, u32[]{:S(2)}, u32[]{:S(2)}) collective-permute-start(bf16[160,1024]{1,0:T(8,128)(2,1)S(1)} %get-tuple-element.258), channel_id=1, source_target_pairs={{0,24},{4,28},{8,16},{12,20},{16,8},{20,12},{24,0},{28,4},{1,25},{... | collective-permute-start | bytes 983048 | tf_op jit(solution)/shard_map/ppermute | solution.py:706
  428.6 26.2 %copy-start.41 = (f32[256,1024]{1,0:T(8,128)S(1)}, f32[256,1024]{1,0:T(8,128)}, u32[]{:S(2)}) copy-start(f32[256,1024]{1,0:T(8,128)} %get-tuple-element.148) | copy-start | bytes 3145732
  428.7 14.9 %collective-permute-start.39 = (bf16[64,1536]{1,0:T(8,128)(2,1)S(1)}, bf16[64,1536]{1,0:T(8,128)(2,1)S(1)}, u32[]{:S(2)}, u32[]{:S(2)}) collective-permute-start(bf16[64,1536]{1,0:T(8,128)(2,1)S(1)} %get-tuple-element.263), channel_id=1, source_target_pairs={{0,8},{4,12},{8,0},{12,4},{16,24},{20,28},{24,16},{28,20},{1,9},{5... | collective-permute-start | bytes 589832 | tf_op jit(solution)/shard_map/ppermute | solution.py:706
  436.0 17.2 %collective-permute-start.40 = (bf16[64,1536]{1,0:T(8,128)(2,1)S(1)}, bf16[64,1536]{1,0:T(8,128)(2,1)S(1)}, u32[]{:S(2)}, u32[]{:S(2)}) collective-permute-start(bf16[64,1536]{1,0:T(8,128)(2,1)S(1)} %get-tuple-element.264), channel_id=1, source_target_pairs={{0,16},{4,20},{8,24},{12,28},{16,0},{20,4},{24,8},{28,12},{1,17},{... | collective-permute-start | bytes 589832 | tf_op jit(solution)/shard_map/ppermute | solution.py:706
  436.0 17.1 %collective-permute-start.41 = (bf16[64,1536]{1,0:T(8,128)(2,1)S(1)}, bf16[64,1536]{1,0:T(8,128)(2,1)S(1)}, u32[]{:S(2)}, u32[]{:S(2)}) collective-permute-start(bf16[64,1536]{1,0:T(8,128)(2,1)S(1)} %get-tuple-element.265), channel_id=1, source_target_pairs={{0,24},{4,28},{8,16},{12,20},{16,8},{20,12},{24,0},{28,4},{1,25},{... | collective-permute-start | bytes 589832 | tf_op jit(solution)/shard_map/ppermute | solution.py:706
  438.4 16.4 %collective-permute-start.38 = (bf16[128,1024]{1,0:T(8,128)(2,1)S(1)}, bf16[128,1024]{1,0:T(8,128)(2,1)S(1)}, u32[]{:S(2)}, u32[]{:S(2)}) collective-permute-start(bf16[128,1024]{1,0:T(8,128)(2,1)S(1)} %slice.274), channel_id=1, source_target_pairs={{0,2},{1,3},{2,0},{3,1},{4,6},{5,7},{6,4},{7,5},{8,10},{9,11},{10,... | collective-permute-start | bytes 786440 | tf_op jit(solution)/shard_map/ppermute | solution.py:706
  440.0 18.3 %collective-permute-start.44 = (f32[32,2048]{1,0:T(8,128)S(1)}, f32[32,2048]{1,0:T(8,128)S(1)}, u32[]{:S(2)}, u32[]{:S(2)}) collective-permute-start(f32[32,2048]{1,0:T(8,128)S(1)} %broadcast_select_fusion.2), channel_id=1, source_target_pairs={{0,1},{1,0},{2,3},{3,2},{4,5},{5,4},{6,7},{7,6},{8,9},{9,8},{10,11... | collective-permute-start | bytes 786440 | tf_op jit(solution)/shard_map/ppermute | solution.py:706
  453.3 6.8 %collective-permute-start.42 = (f32[32,1536]{1,0:T(8,128)S(1)}, f32[32,1536]{1,0:T(8,128)S(1)}, u32[]{:S(2)}, u32[]{:S(2)}) collective-permute-start(f32[32,1536]{1,0:T(8,128)S(1)} %slice.230), channel_id=1, source_target_pairs={{0,2},{1,3},{2,0},{3,1},{4,6},{5,7},{6,4},{7,5},{8,10},{9,11},{10,... | collective-permute-start | bytes 589832 | tf_op jit(solution)/shard_map/ppermute | solution.py:706
  (76 other events, 604.8 us)
Sparse Core Ops, SparseCore 0:
  11.4 161.1 all-gather.2
where the time goes:
time: 480 us; the launch traced here: 472 us
  Pallas kernels  153 us (32%)
  waiting for transfers between devices  114 us (24%)
  starting transfers between devices  103 us (21%)
  local copies, waits for them, and re-layouts  32.8 us (7%)
  other arithmetic  30.1 us (6%)
  matrix products  21.8 us (5%)
  between operations  17.3 us (4%)
    ppermute x45, waiting for transfers between devices, trade(): return lax.ppermute(block, axis, [(i, i ^ bit) for i in range(size)])  67.3 us
    ppermute x45, starting transfers between devices, trade(): return lax.ppermute(block, axis, [(i, i ^ bit) for i in range(size)])  58.3 us
    pallas_call x2, Pallas kernels, attend_back(): pl.pallas_call(functools.partial(attend_back_kernel, chips, bool(sums), s...  56.5 us
    all_to_all x4, waiting for transfers between devices, exchanged(): lax.all_to_all(block, 'head', split_axis=0, concat_axis=0, tiled=True)  44.9 us
    pallas_call x2, Pallas kernels, attend(): pl.pallas_call(functools.partial(attend_kernel, chips), name='attend', ou...  36 us
    all_to_all x4, starting transfers between devices, exchanged(): lax.all_to_all(block, 'head', split_axis=0, concat_axis=0, tiled=True)  21.8 us
    dot_general x7, matrix products, dot_on(): lax.dot_general(left, right, (((left_dim,), (right_dim,)), ((), ())), pre...  18.4 us
    all_to_all x3, starting transfers between devices, exchanged_all(): lax.all_to_all(block, ('head', 'blk'), split_axis=0, concat_axis=0, tiled...  17.2 us
  transfers between devices with their start and end apart: 54, of which 21 were waited for; matrix products, arithmetic and copies ran while one was open for 12% of the time, Pallas kernels for 27%

commit v1 on v0

--- a/solution.py
+++ b/solution.py
@@ -357,7 +357,7 @@
 
 TQ = 512
 KT = 512
-MARGIN = 256
+MARGIN = 128
 AUG = 80
 NT = (((1,), (1,)), ((), ()))
 
@@ -394,7 +394,7 @@
     whole = (key_at >= last_start) & (key_at + KT <= first_end)
     plain = whole & ((gap + KT <= -MAXREL + 1) | (gap >= TQ + MAXREL - 1))
     strip_at = jnp.clip(gap, -(KT + MARGIN), TQ + MARGIN) + KT + MARGIN
-    return touched, plain, gap, pl.ds(pl.multiple_of(strip_at, 256), KT)
+    return touched, plain, gap, pl.ds(pl.multiple_of(strip_at, 128), KT)
 
 
 def masked(scores, bias, key_at, start_row, end_row):
@@ -459,7 +459,7 @@
 
                     @pl.when(touched & jnp.logical_not(plain))
                     def _():
-                        take(masked(raw(), bias_ref[strip, :], key_at, start_row, end_row), 0.0, block, key_tile)
+                        take(masked(raw(), bias_ref[strip, :].astype(jnp.float32), key_at, start_row, end_row), 0.0, block, key_tile)
 
                     return 0
 
@@ -556,7 +556,7 @@
                     @pl.when(touched & jnp.logical_not(plain))
                     def _():
                         whole_grad, _ = take(
-                            masked(raw(), bias_ref[strip, :], key_at, start_row, end_row), 0.0, block, key_tile
+                            masked(raw(), bias_ref[strip, :].astype(jnp.float32), key_at, start_row, end_row), 0.0, block, key_tile
                         )
                         band_ref[strip, :] += whole_grad
 
@@ -589,20 +589,20 @@
 def strip_kernel(far_ref, wave_ref, strip_ref):
     near_blocks, _, width = wave_ref.shape
     first = KT + MARGIN - 128
-    strip_ref[:first, :] = jnp.full((first, TQ), far_ref[0], jnp.float32)
+    strip_ref[:first, :] = jnp.full((first, TQ), far_ref[0], jnp.float32).astype(jnp.bfloat16)
     for k in range(near_blocks):
         spread = jnp.broadcast_to(wave_ref[k], (128, width))
         turned = pltpu.roll(spread, 0, 1, stride=1, stride_axis=0)
-        strip_ref[first + 128 * k : first + 128 * (k + 1), :] = turned[:, :TQ]
+        strip_ref[first + 128 * k : first + 128 * (k + 1), :] = turned[:, :TQ].astype(jnp.bfloat16)
     last = first + 128 * near_blocks
-    strip_ref[last:, :] = jnp.full((strip_ref.shape[0] - last, TQ), far_ref[1], jnp.float32)
+    strip_ref[last:, :] = jnp.full((strip_ref.shape[0] - last, TQ), far_ref[1], jnp.float32).astype(jnp.bfloat16)
 
 
 def bias_strip(far_bias, waves):
     return pl.pallas_call(
         strip_kernel,
         name="bias_strip",
-        out_shape=jax.ShapeDtypeStruct((2 * KT + 2 * MARGIN + TQ, TQ), jnp.float32),
+        out_shape=jax.ShapeDtypeStruct((2 * KT + 2 * MARGIN + TQ, TQ), jnp.bfloat16),
         in_specs=[SMEM, VMEM],
         out_specs=VMEM,
         compiler_params=pltpu.CompilerParams(vmem_limit_bytes=32 * 2**20),
@@ -1333,7 +1333,7 @@
     in_sent = column_sent(after(in_parts, made[1]))
     got = mate(given)
     by_y = across_y((wide(by_y) + wide(got[column:])).astype(low))
-    by_y, in_sent = beside(by_y, in_sent)
+    by_y, in_sent[1] = beside(by_y, in_sent[1])
     first_sent = column_sent((near, got[:column], by_y))
     first_sum = column_total(first_sent)
     first_sums = [first_sum[:shard], across_x(first_sum[shard:])]

time: 480 us -> 480 us (level)
  transfers between devices with their start and end apart: 54 -> 54, of which waited for: 21 -> 21; matrix products, arithmetic and copies ran while one was open for 12% -> 13% of each run, Pallas kernels for 27% -> 27%
where the time goes in v1:
time: 480 us; the launch traced here: 471 us
  Pallas kernels  149 us (31%)
  waiting for transfers between devices  113 us (24%)
  starting transfers between devices  106 us (22%)
  local copies, waits for them, and re-layouts  34 us (7%)
  other arithmetic  31.2 us (6%)
  matrix products  21.8 us (5%)
  between operations  16.9 us (4%)
    ppermute x45, waiting for transfers between devices, trade(): return lax.ppermute(block, axis, [(i, i ^ bit) for i in range(size)])  68.2 us
    ppermute x45, starting transfers between devices, trade(): return lax.ppermute(block, axis, [(i, i ^ bit) for i in range(size)])  59.9 us
    pallas_call x2, Pallas kernels, attend_back(): pl.pallas_call(functools.partial(attend_back_kernel, chips, bool(sums), s...  54.9 us
    all_to_all x4, waiting for transfers between devices, exchanged(): lax.all_to_all(block, 'head', split_axis=0, concat_axis=0, tiled=True)  44 us
    pallas_call x2, Pallas kernels, attend(): pl.pallas_call(functools.partial(attend_kernel, chips), name='attend', ou...  33.5 us
    all_to_all x4, starting transfers between devices, exchanged(): lax.all_to_all(block, 'head', split_axis=0, concat_axis=0, tiled=True)  24.1 us
    dot_general x7, matrix products, dot_on(): lax.dot_general(left, right, (((left_dim,), (right_dim,)), ((), ())), pre...  18.4 us
    unnamed x182, local copies, waits for them, and re-layouts  17.2 us
  transfers between devices with their start and end apart: 54, of which 21 were waited for; matrix products, arithmetic and copies ran while one was open for 13% of the time, Pallas kernels for 27%

profile of v1, /device:TPU:0, one launch (start us, length us, event | category | flops | bytes accessed | tf_op | source)
XLA Modules:
  0.0 471.1 jit_solution(12505101181145413000)
XLA Ops:
  13.8 5.1 %collective-permute-start.4 = (bf16[32,1536]{1,0:T(8,128)(2,1)S(1)}, bf16[32,1536]{1,0:T(8,128)(2,1)S(1)}, u32[]{:S(2)}, u32[]{:S(2)}) collective-permute-start(bf16[32,1536]{1,0:T(8,128)(2,1)S(1)} %select_n.164), channel_id=1, source_target_pairs={{0,24},{4,28},{8,16},{12,20},{16,8},{20,12},{24,0},{28,4},{1,25},{... | collective-permute-start | bytes 294920 | tf_op jit(solution)/shard_map/ppermute | solution.py:706
  19.8 1.7 collective-permute-start.1
  25.5 2.3 collective-permute-done.3
  27.8 10.3 %collective-permute-start.9 = (bf16[32,1536]{1,0:T(8,128)(2,1)S(1)}, bf16[32,1536]{1,0:T(8,128)(2,1)}, u32[]{:S(2)}, u32[]{:S(2)}) collective-permute-start(bf16[32,1536]{1,0:T(8,128)(2,1)S(1)} %collective-permute-done.1), channel_id=1, source_target_pairs={{0,24},{4,28},{8,16},{12,20},{16,8},{20,12},{24,0},{28,4},{1,25},{... | collective-permute-start | bytes 294920 | tf_op jit(solution)/shard_map/ppermute | solution.py:706
  40.7 5.2 %all-to-all-start = ((bf16[32,8,128]{2,1,0:T(8,128)(2,1)}), bf16[32,8,128]{2,1,0:T(8,128)(2,1)}, u32[]{:S(2)}, u32[]{:S(2)}) async-start(bf16[32,8,128]{2,1,0:T(8,128)(2,1)} %broadcast_in_dim.81), calls=%async_computation | async-start | bytes 131072 | tf_op jit(solution)/shard_map/all_to_all | solution.py:1193
  46.0 2.4 collective-permute-done.8
  48.4 1.8 pad_maximum_fusion.6
  56.9 2.7 normed_by_seq.1
  59.6 6.4 %collective-permute-done.10 = bf16[128,1536]{1,0:T(8,128)(2,1)} collective-permute-done((bf16[128,1536]{1,0:T(8,128)(2,1)}, bf16[128,1536]{1,0:T(8,128)(2,1)}, u32[]{:S(2)}, u32[]{:S(2)}) %collective-permute-start.10) | collective-permute-done | bytes 393248 | tf_op jit(solution)/shard_map/ppermute | solution.py:706
  67.4 2.0 collective-permute-done.11.arrays_3_
  69.5 2.4 whole_first.1
  71.9 3.9 convolution_convert_fusion.1
  75.7 5.7 %all-to-all-start.1 = ((bf16[8,192,256]{2,1,0:T(8,128)(2,1)}), bf16[8,192,256]{2,1,0:T(8,128)(2,1)S(1)}, u32[]{:S(2)}, u32[]{:S(2)}) async-start(bf16[8,192,256]{2,1,0:T(8,128)(2,1)} %bitcast.7), calls=%async_computation.1 | async-start | bytes 1572864 | tf_op jit(solution)/shard_map/all_to_all | solution.py:1180
  86.3 28.7 %all-to-all-done.1.refs_0_ = bf16[8,192,256]{2,1,0:T(8,128)(2,1)S(1)} async-done(((bf16[8,192,256]{2,1,0:T(8,128)(2,1)}), bf16[8,192,256]{2,1,0:T(8,128)(2,1)S(1)}, u32[]{:S(2)}, u32[]{:S(2)}) %all-to-all-start.1) | async-done | bytes 786464 | tf_op jit(solution)/shard_map/all_to_all | solution.py:1180
  114.9 4.2 convolution_convert_fusion
  120.1 5.8 %all-to-all-start.2 = ((bf16[8,192,256]{2,1,0:T(8,128)(2,1)}), bf16[8,192,256]{2,1,0:T(8,128)(2,1)S(1)}, u32[]{:S(2)}, u32[]{:S(2)}) async-start(bf16[8,192,256]{2,1,0:T(8,128)(2,1)} %bitcast.127), calls=%async_computation.2 | async-start | bytes 1572864 | tf_op jit(solution)/shard_map/all_to_all | solution.py:1180
  128.4 22.4 %attend.2 = (f32[8,64,256]{2,1,0:T(8,128)S(1)}, bf16[16,64,128]{2,1,0:T(8,128)(2,1)}, f32[2,1,2,512]{3,2,1,0:T(2,128)S(1)}) custom-call(s32[5]{0:T(128)S(1)} %pad_add_fusion.2.base_ref, s32[16]{0:T(128)S(1)} %reshape_squeeze.7.edge_ref, f32[2]{0:T(128)S(1)} %pad_maximum_fusion.12.far_ref, bf16[8,192,256]{2,1,0:T(8,128)(2,1)S(1)} %copy-done.5, ...), custom_call_target="tpu_custom_call" | custom-call | flops 1 | bytes 1 | tf_op jit(solution)/shard_map/attend/pallas_call | solution.py:655
  152.2 12.1 %all-to-all-done.2.refs_0_ = bf16[8,192,256]{2,1,0:T(8,128)(2,1)S(1)} async-done(((bf16[8,192,256]{2,1,0:T(8,128)(2,1)}), bf16[8,192,256]{2,1,0:T(8,128)(2,1)S(1)}, u32[]{:S(2)}, u32[]{:S(2)}) %all-to-all-start.2) | async-done | bytes 786464 | tf_op jit(solution)/shard_map/all_to_all | solution.py:1180
  164.6 3.7 all-to-all-start.3
  168.3 11.0 %attend.3 = (f32[8,64,256]{2,1,0:T(8,128)S(1)}, bf16[16,64,128]{2,1,0:T(8,128)(2,1)}, f32[2,1,2,512]{3,2,1,0:T(2,128)S(1)}) custom-call(s32[5]{0:T(128)S(1)} %pad_add_fusion.2.base_ref, s32[16]{0:T(128)S(1)} %reshape_squeeze.6.edge_ref, f32[2]{0:T(128)S(1)} %pad_maximum_fusion.12.far_ref, bf16[8,192,256]{2,1,0:T(8,128)(2,1)S(1)} %all-to-all-done.2.refs_0_, ...), custom_call_target="tpu_custom_call" | custom-call | flops 1 | bytes 1 | tf_op jit(solution)/shard_map/attend/pallas_call | solution.py:655
  180.8 6.9 %all-to-all-start.4 = ((bf16[16,64,128]{2,1,0:T(8,128)(2,1)}), bf16[16,64,128]{2,1,0:T(8,128)(2,1)S(1)}, u32[]{:S(2)}, u32[]{:S(2)}) async-start(bf16[16,64,128]{2,1,0:T(8,128)(2,1)} %get-tuple-element.170), calls=%async_computation.4 | async-start | bytes 524288 | tf_op jit(solution)/shard_map/all_to_all | solution.py:1177
  189.3 8.2 %own_halves.1 = (bf16[1024,2048]{1,0:T(8,128)(2,1)}, bf16[1024,1024]{1,0:T(8,128)(2,1)}, bf16[2048,1024]{1,0:T(8,128)(2,1)}) custom-call(s32[1]{0:T(128)} %bitcast.16.place_ref, bf16[32,288,1024]{2,1,0:T(8,128)(2,1)} %bitcast.106, bf16[32,288,1024]{2,1,0:T(8,128)(2,1)} %bitcast.107, bf16[32,288,1024]{2,1,0:T(8,128)(2,1)} %bitcast.108, ...), custom_call_target="tpu_custom_call" | custom-call | tf_op jit(solution)/shard_map/own_halves/pallas_call | solution.py:1041
  197.7 2.6 multiply_reduce_fusion.2
  201.3 1.7 pad_maximum_fusion.1.grad_ref.right_ref
  203.1 14.2 %feed.1 = (bf16[512,2048]{1,0:T(8,128)(2,1)}, bf16[512,2048]{1,0:T(8,128)(2,1)}, f32[256,1024]{1,0:T(8,128)}, f32[256,1024]{1,0:T(8,128)}, f32[256,1024]{1,0:T(8,128)}, /*index=5*/f32[256,1024]{1,0:T(8,128)}) custom-call(bf16[512,1024]{1,0:T(8,128)(2,1)S(1)} %pad_maximum_fusion.rows_ref.left_ref, bf16[512,1024]{1,0:T(8,128)(2,1)S(1)} %pad_maximum_fusion.1.grad_ref.right_ref, ...), custom_call_target="tpu_custom_call" | custom-call | flops 1 | bytes 1 | tf_op jit(solution)/shard_map/feed/pallas_call | solution.py:929
  217.9 4.7 %weight_grad.2.arrays_0_ = bf16[2048,1024]{1,0:T(8,128)(2,1)S(1)} custom-call(bf16[512,2048]{1,0:T(8,128)(2,1)} %get-tuple-element.183.left_ref, bf16[512,1024]{1,0:T(8,128)(2,1)} %copy-done.2), custom_call_target="tpu_custom_call" | custom-call | flops 1 | bytes 1 | tf_op jit(solution)/shard_map/weight_grad/pallas_call | solution.py:955
  222.6 2.9 parts_down.1
  225.5 1.9 collective-permute-start.18
  229.2 3.0 fusion.21
  233.8 6.3 %collective-permute-done.18.part_ref = bf16[256,1024]{1,0:T(8,128)(2,1)S(1)} collective-permute-done((bf16[256,1024]{1,0:T(8,128)(2,1)}, bf16[256,1024]{1,0:T(8,128)(2,1)S(1)}, u32[]{:S(2)}, u32[]{:S(2)}) %collective-permute-start.18) | collective-permute-done | bytes 524320 | tf_op jit(solution)/shard_map/ppermute | solution.py:706
  244.7 6.0 %all-to-all-start.5 = ((bf16[16,64,256]{2,1,0:T(8,128)(2,1)}), bf16[16,64,256]{2,1,0:T(8,128)(2,1)}, u32[]{:S(2)}, u32[]{:S(2)}) async-start(bf16[16,64,256]{2,1,0:T(8,128)(2,1)} %bitcast.128), calls=%async_computation.5 | async-start | bytes 1048576 | tf_op jit(solution)/shard_map/all_to_all | solution.py:1177
  251.9 2.0 collective-permute-start.23
  256.6 4.5 weight_grad.3.arrays_0_
  261.1 1.9 fusion.2
  263.0 3.2 parts_in.1
  268.0 34.8 %attend_back.2 = (bf16[8,192,256]{2,1,0:T(8,128)(2,1)}, bf16[8,128,256]{2,1,0:T(8,128)(2,1)}, f32[1792,512]{1,0:T(8,128)}, f32[8,512]{1,0:T(8,128)}) custom-call(s32[5]{0:T(128)} %copy-done.34, s32[16]{0:T(128)} %copy-done.36, f32[2]{0:T(128)} %copy-done.31, bf16[16,64,256]{2,1,0:T(8,128)(2,1)} %all-to-all-done.5.g_ref, f32[8,64,256]{2,1,0:T(8,128)} %copy-done.25, ...), custom_call_target="tpu_custom_call" | custom-call | flops 1 | bytes 1 | tf_op jit(solution)/shard_map/attend_back/pallas_call | solution.py:681
  304.6 2.1 collective-permute-done.25.part_ref
  309.0 5.1 %all-to-all-start.6 = ((bf16[8,192,256]{2,1,0:T(8,128)(2,1)}), bf16[8,192,256]{2,1,0:T(8,128)(2,1)}, u32[]{:S(2)}, u32[]{:S(2)}) async-start(bf16[8,192,256]{2,1,0:T(8,128)(2,1)} %added.8), calls=%async_computation.6 | async-start | bytes 1572864 | tf_op jit(solution)/shard_map/all_to_all | solution.py:1180
  315.4 2.1 collective-permute-start.27
  319.2 1.6 column.3
  322.3 2.4 collective-permute-start.29
  325.2 20.1 %attend_back.3 = (bf16[8,192,256]{2,1,0:T(8,128)(2,1)}, bf16[8,128,256]{2,1,0:T(8,128)(2,1)}, f32[1792,512]{1,0:T(8,128)}, f32[8,512]{1,0:T(8,128)}) custom-call(s32[5]{0:T(128)} %copy-done.34, s32[16]{0:T(128)} %copy-done.35, f32[2]{0:T(128)} %copy-done.31, bf16[16,64,256]{2,1,0:T(8,128)(2,1)} %all-to-all-done.5.g_ref, f32[8,64,256]{2,1,0:T(8,128)} %copy-done.24, ...), custom_call_target="tpu_custom_call" | custom-call | flops 1 | bytes 1 | tf_op jit(solution)/shard_map/attend_back/pallas_call | solution.py:681
  345.4 7.0 %collective-permute-done.29 = bf16[128,1024]{1,0:T(8,128)(2,1)S(1)} collective-permute-done((bf16[128,1024]{1,0:T(8,128)(2,1)S(1)}, bf16[128,1024]{1,0:T(8,128)(2,1)S(1)}, u32[]{:S(2)}, u32[]{:S(2)}) %collective-permute-start.29) | collective-permute-done | bytes 262176 | tf_op jit(solution)/shard_map/ppermute | solution.py:706
  353.3 2.1 collective-permute-done.31.part_ref
  357.6 7.5 %all-to-all-start.7 = ((bf16[8,192,256]{2,1,0:T(8,128)(2,1)}), bf16[8,192,256]{2,1,0:T(8,128)(2,1)}, u32[]{:S(2)}, u32[]{:S(2)}) async-start(bf16[8,192,256]{2,1,0:T(8,128)(2,1)} %added.11), calls=%async_computation.7 | async-start | bytes 1572864 | tf_op jit(solution)/shard_map/all_to_all | solution.py:1180
  365.1 2.0 copy.129
  367.2 2.0 copy.130
  369.2 3.3 fusion.36
  375.1 2.4 band_sums.1
  378.2 2.0 fusion.5
  382.0 3.2 all-to-all-done.7
  385.2 5.3 %first_back.1 = (bf16[512,1536]{1,0:T(8,128)(2,1)}, bf16[256,1536]{1,0:T(8,128)(2,1)}, bf16[256,1536]{1,0:T(8,128)(2,1)}) custom-call(s32[64]{0:T(128)S(1)} %pad_add_fusion.3.slots_ref, bf16[1024,256]{1,0:T(8,128)(2,1)} %bitcast.122, bf16[1536,256]{1,0:T(8,128)(2,1)} %bitcast.31.made_0, bf16[1024,256]{1,0:T(8,128)(2,1)} %bitcast.123, ...), custom_call_target="tpu_custom_call" | custom-call | tf_op jit(solution)/shard_map/first_back/pallas_call | solution.py:984
  391.7 2.5 collective-permute-done.33
  394.2 1.6 add_convert_fusion
  399.9 2.0 collective-permute-start.41
  401.9 2.4 collective-permute-start.42
  406.0 9.8 %collective-permute-done.35 = bf16[160,1024]{1,0:T(8,128)(2,1)S(1)} collective-permute-done((bf16[160,1024]{1,0:T(8,128)(2,1)S(1)}, bf16[160,1024]{1,0:T(8,128)(2,1)S(1)}, u32[]{:S(2)}, u32[]{:S(2)}) %collective-permute-start.35) | collective-permute-done | bytes 327712 | tf_op jit(solution)/shard_map/ppermute | solution.py:706
  416.1 9.4 %collective-permute-done.41 = bf16[160,1024]{1,0:T(8,128)(2,1)S(1)} collective-permute-done((bf16[160,1024]{1,0:T(8,128)(2,1)S(1)}, bf16[160,1024]{1,0:T(8,128)(2,1)S(1)}, u32[]{:S(2)}, u32[]{:S(2)}) %collective-permute-start.41) | collective-permute-done | bytes 327712 | tf_op jit(solution)/shard_map/ppermute | solution.py:706
  426.4 2.2 fusion.37
  428.6 7.2 %collective-permute-start.37 = (bf16[64,1536]{1,0:T(8,128)(2,1)S(1)}, bf16[64,1536]{1,0:T(8,128)(2,1)S(1)}, u32[]{:S(2)}, u32[]{:S(2)}) collective-permute-start(bf16[64,1536]{1,0:T(8,128)(2,1)S(1)} %get-tuple-element.257), channel_id=1, source_target_pairs={{0,8},{4,12},{8,0},{12,4},{16,24},{20,28},{24,16},{28,20},{1,9},{5... | collective-permute-start | bytes 589832 | tf_op jit(solution)/shard_map/ppermute | solution.py:706
  435.9 2.4 collective-permute-start.39
  439.9 3.6 collective-permute-done.37
  443.5 9.5 %collective-permute-done.38 = bf16[64,1536]{1,0:T(8,128)(2,1)S(1)} collective-permute-done((bf16[64,1536]{1,0:T(8,128)(2,1)S(1)}, bf16[64,1536]{1,0:T(8,128)(2,1)S(1)}, u32[]{:S(2)}, u32[]{:S(2)}) %collective-permute-start.38) | collective-permute-done | bytes 196640 | tf_op jit(solution)/shard_map/ppermute | solution.py:706
  460.7 2.0 by_weight.1
  (372 shorter events, 84.9 us)
Async XLA Ops:
  7.2 182.1 %all-gather.3.cloned.1.call-start = ((), (), s32[]{:S(2)}) async-start(), calls=%async_computation.8 | async-start | bytes 19464192 | tf_op jit(solution)/shard_map/all_gather | solution.py:1225
  13.8 11.7 %collective-permute-start.4 = (bf16[32,1536]{1,0:T(8,128)(2,1)S(1)}, bf16[32,1536]{1,0:T(8,128)(2,1)S(1)}, u32[]{:S(2)}, u32[]{:S(2)}) collective-permute-start(bf16[32,1536]{1,0:T(8,128)(2,1)S(1)} %select_n.164), channel_id=1, source_target_pairs={{0,24},{4,28},{8,16},{12,20},{16,8},{20,12},{24,0},{28,4},{1,25},{... | collective-permute-start | bytes 294920 | tf_op jit(solution)/shard_map/ppermute | solution.py:706
  18.9 8.8 %collective-permute-start.3 = (bf16[32,1536]{1,0:T(8,128)(2,1)S(1)}, bf16[32,1536]{1,0:T(8,128)(2,1)S(1)}, u32[]{:S(2)}, u32[]{:S(2)}) collective-permute-start(bf16[32,1536]{1,0:T(8,128)(2,1)S(1)} %select_n.164), channel_id=1, source_target_pairs={{0,16},{4,20},{8,24},{12,28},{16,0},{20,4},{24,8},{28,12},{1,17},{... | collective-permute-start | bytes 294920 | tf_op jit(solution)/shard_map/ppermute | solution.py:706
  18.9 8.8 %collective-permute-start.2 = (bf16[32,1536]{1,0:T(8,128)(2,1)S(1)}, bf16[32,1536]{1,0:T(8,128)(2,1)S(1)}, u32[]{:S(2)}, u32[]{:S(2)}) collective-permute-start(bf16[32,1536]{1,0:T(8,128)(2,1)S(1)} %select_n.164), channel_id=1, source_target_pairs={{0,8},{4,12},{8,0},{12,4},{16,24},{20,28},{24,16},{28,20},{1,9},{5... | collective-permute-start | bytes 294920 | tf_op jit(solution)/shard_map/ppermute | solution.py:706
  19.8 8.0 %collective-permute-start.1 = (bf16[32,1536]{1,0:T(8,128)(2,1)S(1)}, bf16[32,1536]{1,0:T(8,128)(2,1)S(1)}, u32[]{:S(2)}, u32[]{:S(2)}) collective-permute-start(bf16[32,1536]{1,0:T(8,128)(2,1)S(1)} %select_n.161), channel_id=1, source_target_pairs={{0,2},{1,3},{2,0},{3,1},{4,6},{5,7},{6,4},{7,5},{8,10},{9,11},{10,... | collective-permute-start | bytes 294920 | tf_op jit(solution)/shard_map/ppermute | solution.py:706
  23.6 32.6 %collective-permute-start = (bf16[2,128,1024]{2,1,0:T(8,128)(2,1)S(1)}, bf16[2,128,1024]{2,1,0:T(8,128)(2,1)S(1)}, u32[]{:S(2)}, u32[]{:S(2)}) collective-permute-start(bf16[2,128,1024]{2,1,0:T(8,128)(2,1)S(1)} %fusion.7.here_ref), channel_id=1, source_target_pairs={{0,2},{1,3},{2,0},{3,1},{4,6},{5,7},{6,4},{7,5},{8,10},{9,11},{10,... | collective-permute-start | bytes 1572872 | tf_op jit(solution)/shard_map/ppermute | solution.py:706
  27.8 18.2 %collective-permute-start.9 = (bf16[32,1536]{1,0:T(8,128)(2,1)S(1)}, bf16[32,1536]{1,0:T(8,128)(2,1)}, u32[]{:S(2)}, u32[]{:S(2)}) collective-permute-start(bf16[32,1536]{1,0:T(8,128)(2,1)S(1)} %collective-permute-done.1), channel_id=1, source_target_pairs={{0,24},{4,28},{8,16},{12,20},{16,8},{20,12},{24,0},{28,4},{1,25},{... | collective-permute-start | bytes 294920 | tf_op jit(solution)/shard_map/ppermute | solution.py:706
  38.0 10.3 %collective-permute-start.8 = (bf16[32,1536]{1,0:T(8,128)(2,1)S(1)}, bf16[32,1536]{1,0:T(8,128)(2,1)}, u32[]{:S(2)}, u32[]{:S(2)}) collective-permute-start(bf16[32,1536]{1,0:T(8,128)(2,1)S(1)} %collective-permute-done.1), channel_id=1, source_target_pairs={{0,16},{4,20},{8,24},{12,28},{16,0},{20,4},{24,8},{28,12},{1,17},{... | collective-permute-start | bytes 294920 | tf_op jit(solution)/shard_map/ppermute | solution.py:706
  38.0 10.3 %collective-permute-start.7 = (bf16[32,1536]{1,0:T(8,128)(2,1)S(1)}, bf16[32,1536]{1,0:T(8,128)(2,1)}, u32[]{:S(2)}, u32[]{:S(2)}) collective-permute-start(bf16[32,1536]{1,0:T(8,128)(2,1)S(1)} %collective-permute-done.1), channel_id=1, source_target_pairs={{0,8},{4,12},{8,0},{12,4},{16,24},{20,28},{24,16},{28,20},{1,9},{5... | collective-permute-start | bytes 294920 | tf_op jit(solution)/shard_map/ppermute | solution.py:706
  38.7 17.3 %collective-permute-start.5 = (bf16[128,1536]{1,0:T(8,128)(2,1)S(1)}, bf16[128,1536]{1,0:T(8,128)(2,1)S(1)}, u32[]{:S(2)}, u32[]{:S(2)}) collective-permute-start(bf16[128,1536]{1,0:T(8,128)(2,1)S(1)} %pad_maximum_fusion.5), channel_id=1, source_target_pairs={{0,4},{4,0},{8,12},{12,8},{16,20},{20,16},{24,28},{28,24},{1,5},{5... | collective-permute-start | bytes 1179656 | tf_op jit(solution)/shard_map/ppermute | solution.py:706
  40.7 13.7 %all-to-all-start = ((bf16[32,8,128]{2,1,0:T(8,128)(2,1)}), bf16[32,8,128]{2,1,0:T(8,128)(2,1)}, u32[]{:S(2)}, u32[]{:S(2)}) async-start(bf16[32,8,128]{2,1,0:T(8,128)(2,1)} %broadcast_in_dim.81), calls=%async_computation | async-start | bytes 131072 | tf_op jit(solution)/shard_map/all_to_all | solution.py:1193
  50.1 15.9 %collective-permute-start.10 = (bf16[128,1536]{1,0:T(8,128)(2,1)}, bf16[128,1536]{1,0:T(8,128)(2,1)}, u32[]{:S(2)}, u32[]{:S(2)}) collective-permute-start(bf16[128,1536]{1,0:T(8,128)(2,1)} %pad_maximum_fusion.6), channel_id=1, source_target_pairs={{0,4},{4,0},{8,12},{12,8},{16,20},{20,16},{24,28},{28,24},{1,5},{5... | collective-permute-start | bytes 1179656 | tf_op jit(solution)/shard_map/ppermute | solution.py:706
  56.1 11.4 %collective-permute-start.6 = (bf16[256,1536]{1,0:T(8,128)(2,1)S(1)}, bf16[256,1536]{1,0:T(8,128)(2,1)S(1)}, u32[]{:S(2)}, u32[]{:S(2)}) collective-permute-start(bf16[256,1536]{1,0:T(8,128)(2,1)S(1)} %constant_dynamic-update-slice_fusion.arrays_0_), channel_id=1, source_target_pairs={{0,1},{1,0},{2,3},{3,2},{4,5},{5,4},{6,7},{7,6},{8,9},{9,8},{10,11... | collective-permute-start | bytes 2359304 | tf_op jit(solution)/shard_map/ppermute | solution.py:706
  67.1 2.4 collective-permute-start.11
  75.7 39.2 %copy-start.60 = (bf16[256,1024]{1,0:T(8,128)(2,1)S(1)}, bf16[256,1024]{1,0:T(8,128)(2,1)}, u32[]{:S(2)}) copy-start(bf16[256,1024]{1,0:T(8,128)(2,1)} %get-tuple-element.155) | copy-start | bytes 1572868
  75.7 39.2 %all-to-all-start.1 = ((bf16[8,192,256]{2,1,0:T(8,128)(2,1)}), bf16[8,192,256]{2,1,0:T(8,128)(2,1)S(1)}, u32[]{:S(2)}, u32[]{:S(2)}) async-start(bf16[8,192,256]{2,1,0:T(8,128)(2,1)} %bitcast.7), calls=%async_computation.1 | async-start | bytes 1572864 | tf_op jit(solution)/shard_map/all_to_all | solution.py:1180
  85.3 83.0 %copy-start.31 = (f32[2]{0:T(128)}, f32[2]{0:T(128)S(1)}, u32[]{:S(2)}) copy-start(f32[2]{0:T(128)S(1)} %pad_maximum_fusion.12.far_ref) | copy-start | bytes 28
  86.3 82.1 %copy-start = (bf16[1792,512]{1,0:T(8,128)(2,1)}, bf16[1792,512]{1,0:T(8,128)(2,1)S(1)}, u32[]{:S(2)}) copy-start(bf16[1792,512]{1,0:T(8,128)(2,1)S(1)} %bias_strip.1.refs_4_) | copy-start | bytes 5505028
  86.3 39.6 %copy-start.85 = (s32[4]{0:T(128)S(1)}, s32[4]{0:T(128)}, u32[]{:S(2)}) copy-start(s32[4]{0:T(128)} %constant.87.clone) | copy-start | bytes 52
  114.9 4.2 collective-permute-start.12
  120.1 44.2 %all-to-all-start.2 = ((bf16[8,192,256]{2,1,0:T(8,128)(2,1)}), bf16[8,192,256]{2,1,0:T(8,128)(2,1)S(1)}, u32[]{:S(2)}, u32[]{:S(2)}) async-start(bf16[8,192,256]{2,1,0:T(8,128)(2,1)} %bitcast.127), calls=%async_computation.2 | async-start | bytes 1572864 | tf_op jit(solution)/shard_map/all_to_all | solution.py:1180
  126.0 53.4 %copy-start.34 = (s32[5]{0:T(128)}, s32[5]{0:T(128)S(1)}, u32[]{:S(2)}) copy-start(s32[5]{0:T(128)S(1)} %pad_add_fusion.2.base_ref) | copy-start | bytes 64
  126.1 53.3 %copy-start.36 = (s32[16]{0:T(128)}, s32[16]{0:T(128)S(1)}, u32[]{:S(2)}) copy-start(s32[16]{0:T(128)S(1)} %reshape_squeeze.7.edge_ref) | copy-start | bytes 196
  126.1 53.3 %copy-start.26 = (s32[2,1,2,512]{3,2,1,0:T(2,128)}, s32[2,1,2,512]{3,2,1,0:T(2,128)S(1)}, u32[]{:S(2)}) copy-start(s32[2,1,2,512]{3,2,1,0:T(2,128)S(1)} %get-tuple-element.389.refs_2_) | copy-start | bytes 24580
  126.1 53.3 %copy-start.28 = (s32[2,1,2,512]{3,2,1,0:T(2,128)}, s32[2,1,2,512]{3,2,1,0:T(2,128)S(1)}, u32[]{:S(2)}) copy-start(s32[2,1,2,512]{3,2,1,0:T(2,128)S(1)} %get-tuple-element.390.refs_2_) | copy-start | bytes 24580
  126.1 53.3 %copy-start.27 = (s32[2,1,2,512]{3,2,1,0:T(2,128)}, s32[2,1,2,512]{3,2,1,0:T(2,128)S(1)}, u32[]{:S(2)}) copy-start(s32[2,1,2,512]{3,2,1,0:T(2,128)S(1)} %get-tuple-element.387.refs_3_) | copy-start | bytes 24580
  126.1 53.3 %copy-start.29 = (s32[2,1,2,512]{3,2,1,0:T(2,128)}, s32[2,1,2,512]{3,2,1,0:T(2,128)S(1)}, u32[]{:S(2)}) copy-start(s32[2,1,2,512]{3,2,1,0:T(2,128)S(1)} %get-tuple-element.388.refs_3_) | copy-start | bytes 24580
  164.3 4.0 collective-permute-start.13
  164.6 16.2 %all-to-all-start.3 = ((bf16[16,64,128]{2,1,0:T(8,128)(2,1)}), bf16[16,64,128]{2,1,0:T(8,128)(2,1)S(1)}, u32[]{:S(2)}, u32[]{:S(2)}) async-start(bf16[16,64,128]{2,1,0:T(8,128)(2,1)} %get-tuple-element.168), calls=%async_computation.3 | async-start | bytes 524288 | tf_op jit(solution)/shard_map/all_to_all | solution.py:1177
  180.8 16.9 %all-to-all-start.4 = ((bf16[16,64,128]{2,1,0:T(8,128)(2,1)}), bf16[16,64,128]{2,1,0:T(8,128)(2,1)S(1)}, u32[]{:S(2)}, u32[]{:S(2)}) async-start(bf16[16,64,128]{2,1,0:T(8,128)(2,1)} %get-tuple-element.170), calls=%async_computation.4 | async-start | bytes 524288 | tf_op jit(solution)/shard_map/all_to_all | solution.py:1177
  189.1 12.1 %collective-permute-start.15 = (bf16[256,1024]{1,0:T(8,128)(2,1)S(1)}, bf16[256,1024]{1,0:T(8,128)(2,1)}, u32[]{:S(2)}, u32[]{:S(2)}) collective-permute-start(bf16[256,1024]{1,0:T(8,128)(2,1)S(1)} %bitcast.114), channel_id=1, source_target_pairs={{0,1},{1,0},{2,3},{3,2},{4,5},{5,4},{6,7},{7,6},{8,9},{9,8},{10,11... | collective-permute-start | bytes 1572872 | tf_op jit(solution)/shard_map/ppermute | solution.py:706
  200.4 2.5 collective-permute-start.14
  217.3 11.6 %collective-permute-start.17 = (f32[256,1024]{1,0:T(8,128)}, f32[256,1024]{1,0:T(8,128)S(1)}, u32[]{:S(2)}, u32[]{:S(2)}) collective-permute-start(f32[256,1024]{1,0:T(8,128)} %get-tuple-element.181), channel_id=1, source_target_pairs={{0,1},{1,0},{2,3},{3,2},{4,5},{5,4},{6,7},{7,6},{8,9},{9,8},{10,11... | collective-permute-start | bytes 3145736 | tf_op jit(solution)/shard_map/ppermute | solution.py:706
  217.7 11.5 %collective-permute-start.16 = (f32[256,1024]{1,0:T(8,128)}, f32[256,1024]{1,0:T(8,128)}, u32[]{:S(2)}, u32[]{:S(2)}) collective-permute-start(f32[256,1024]{1,0:T(8,128)} %get-tuple-element.179), channel_id=1, source_target_pairs={{0,1},{1,0},{2,3},{3,2},{4,5},{5,4},{6,7},{7,6},{8,9},{9,8},{10,11... | collective-permute-start | bytes 3145736 | tf_op jit(solution)/shard_map/ppermute | solution.py:706
  225.5 14.6 %collective-permute-start.18 = (bf16[256,1024]{1,0:T(8,128)(2,1)}, bf16[256,1024]{1,0:T(8,128)(2,1)S(1)}, u32[]{:S(2)}, u32[]{:S(2)}) collective-permute-start(bf16[256,1024]{1,0:T(8,128)(2,1)} %get-tuple-element.187), channel_id=1, source_target_pairs={{0,4},{4,0},{8,12},{12,8},{16,20},{20,16},{24,28},{28,24},{1,5},{5... | collective-permute-start | bytes 1572872 | tf_op jit(solution)/shard_map/ppermute | solution.py:706
  227.4 14.2 %collective-permute-start.19 = (bf16[256,1024]{1,0:T(8,128)(2,1)}, bf16[256,1024]{1,0:T(8,128)(2,1)S(1)}, u32[]{:S(2)}, u32[]{:S(2)}) collective-permute-start(bf16[256,1024]{1,0:T(8,128)(2,1)} %get-tuple-element.188), channel_id=1, source_target_pairs={{0,2},{1,3},{2,0},{3,1},{4,6},{5,7},{6,4},{7,5},{8,10},{9,11},{10,... | collective-permute-start | bytes 1572872 | tf_op jit(solution)/shard_map/ppermute | solution.py:706
  244.7 16.4 %collective-permute-start.20 = (bf16[16,32,1024]{2,1,0:T(8,128)(2,1)}, bf16[16,32,1024]{2,1,0:T(8,128)(2,1)}, u32[]{:S(2)}, u32[]{:S(2)}) collective-permute-start(bf16[16,32,1024]{2,1,0:T(8,128)(2,1)} %select_bitcast_fusion), channel_id=1, source_target_pairs={{0,1},{1,0},{2,3},{3,2},{4,5},{5,4},{6,7},{7,6},{8,9},{9,8},{10,11... | collective-permute-start | bytes 3145736 | tf_op jit(solution)/shard_map/ppermute | solution.py:706
  244.7 21.5 %all-to-all-start.5 = ((bf16[16,64,256]{2,1,0:T(8,128)(2,1)}), bf16[16,64,256]{2,1,0:T(8,128)(2,1)}, u32[]{:S(2)}, u32[]{:S(2)}) async-start(bf16[16,64,256]{2,1,0:T(8,128)(2,1)} %bitcast.128), calls=%async_computation.5 | async-start | bytes 1048576 | tf_op jit(solution)/shard_map/all_to_all | solution.py:1177
  251.9 50.9 %collective-permute-start.23 = (bf16[512,1024]{1,0:T(8,128)(2,1)}, bf16[512,1024]{1,0:T(8,128)(2,1)S(1)}, u32[]{:S(2)}, u32[]{:S(2)}) collective-permute-start(bf16[512,1024]{1,0:T(8,128)(2,1)} %added.6), channel_id=1, source_target_pairs={{0,2},{1,3},{2,0},{3,1},{4,6},{5,7},{6,4},{7,5},{8,10},{9,11},{10,... | collective-permute-start | bytes 3145736 | tf_op jit(solution)/shard_map/ppermute | solution.py:706
  255.1 48.7 %collective-permute-start.24 = (bf16[512,1024]{1,0:T(8,128)(2,1)}, bf16[512,1024]{1,0:T(8,128)(2,1)}, u32[]{:S(2)}, u32[]{:S(2)}) collective-permute-start(bf16[512,1024]{1,0:T(8,128)(2,1)} %added.7), channel_id=1, source_target_pairs={{0,4},{4,0},{8,12},{12,8},{16,20},{20,16},{24,28},{28,24},{1,5},{5... | collective-permute-start | bytes 3145736 | tf_op jit(solution)/shard_map/ppermute | solution.py:706
  266.2 37.6 %collective-permute-start.21 = (bf16[320,1024]{1,0:T(8,128)(2,1)}, bf16[320,1024]{1,0:T(8,128)(2,1)S(1)}, u32[]{:S(2)}, u32[]{:S(2)}) collective-permute-start(bf16[320,1024]{1,0:T(8,128)(2,1)} %get-tuple-element.207), channel_id=1, source_target_pairs={{0,4},{4,0},{8,12},{12,8},{16,20},{20,16},{24,28},{28,24},{1,5},{5... | collective-permute-start | bytes 1966088 | tf_op jit(solution)/shard_map/ppermute | solution.py:706
  267.4 36.4 %collective-permute-start.22 = (bf16[320,1024]{1,0:T(8,128)(2,1)}, bf16[320,1024]{1,0:T(8,128)(2,1)S(1)}, u32[]{:S(2)}, u32[]{:S(2)}) collective-permute-start(bf16[320,1024]{1,0:T(8,128)(2,1)} %get-tuple-element.208), channel_id=1, source_target_pairs={{0,2},{1,3},{2,0},{3,1},{4,6},{5,7},{6,4},{7,5},{8,10},{9,11},{10,... | collective-permute-start | bytes 1966088 | tf_op jit(solution)/shard_map/ppermute | solution.py:706
  304.6 2.1 collective-permute-start.25
  309.0 44.3 %all-to-all-start.6 = ((bf16[8,192,256]{2,1,0:T(8,128)(2,1)}), bf16[8,192,256]{2,1,0:T(8,128)(2,1)}, u32[]{:S(2)}, u32[]{:S(2)}) async-start(bf16[8,192,256]{2,1,0:T(8,128)(2,1)} %added.8), calls=%async_computation.6 | async-start | bytes 1572864 | tf_op jit(solution)/shard_map/all_to_all | solution.py:1180
  315.4 37.8 %collective-permute-start.27 = (bf16[640,1024]{1,0:T(8,128)(2,1)S(1)}, bf16[640,1024]{1,0:T(8,128)(2,1)S(1)}, u32[]{:S(2)}, u32[]{:S(2)}) collective-permute-start(bf16[640,1024]{1,0:T(8,128)(2,1)S(1)} %added.10), channel_id=1, source_target_pairs={{0,4},{4,0},{8,12},{12,8},{16,20},{20,16},{24,28},{28,24},{1,5},{5... | collective-permute-start | bytes 3932168 | tf_op jit(solution)/shard_map/ppermute | solution.py:706
  317.7 35.6 %collective-permute-start.26 = (bf16[640,1024]{1,0:T(8,128)(2,1)S(1)}, bf16[640,1024]{1,0:T(8,128)(2,1)S(1)}, u32[]{:S(2)}, u32[]{:S(2)}) collective-permute-start(bf16[640,1024]{1,0:T(8,128)(2,1)S(1)} %added.9), channel_id=1, source_target_pairs={{0,2},{1,3},{2,0},{3,1},{4,6},{5,7},{6,4},{7,5},{8,10},{9,11},{10,... | collective-permute-start | bytes 3932168 | tf_op jit(solution)/shard_map/ppermute | solution.py:706
  320.8 24.6 %collective-permute-start.28 = (bf16[128,1024]{1,0:T(8,128)(2,1)S(1)}, bf16[128,1024]{1,0:T(8,128)(2,1)S(1)}, u32[]{:S(2)}, u32[]{:S(2)}) collective-permute-start(bf16[128,1024]{1,0:T(8,128)(2,1)S(1)} %get-tuple-element.229), channel_id=1, source_target_pairs={{0,8},{4,12},{8,0},{12,4},{16,24},{20,28},{24,16},{28,20},{1,9},{5... | collective-permute-start | bytes 786440 | tf_op jit(solution)/shard_map/ppermute | solution.py:706
  322.3 30.1 %collective-permute-start.29 = (bf16[128,1024]{1,0:T(8,128)(2,1)S(1)}, bf16[128,1024]{1,0:T(8,128)(2,1)S(1)}, u32[]{:S(2)}, u32[]{:S(2)}) collective-permute-start(bf16[128,1024]{1,0:T(8,128)(2,1)S(1)} %get-tuple-element.230), channel_id=1, source_target_pairs={{0,16},{4,20},{8,24},{12,28},{16,0},{20,4},{24,8},{28,12},{1,17},{... | collective-permute-start | bytes 786440 | tf_op jit(solution)/shard_map/ppermute | solution.py:706
  324.7 27.7 %collective-permute-start.30 = (bf16[128,1024]{1,0:T(8,128)(2,1)S(1)}, bf16[128,1024]{1,0:T(8,128)(2,1)S(1)}, u32[]{:S(2)}, u32[]{:S(2)}) collective-permute-start(bf16[128,1024]{1,0:T(8,128)(2,1)S(1)} %get-tuple-element.231), channel_id=1, source_target_pairs={{0,24},{4,28},{8,16},{12,20},{16,8},{20,12},{24,0},{28,4},{1,25},{... | collective-permute-start | bytes 786440 | tf_op jit(solution)/shard_map/ppermute | solution.py:706
  353.3 2.2 collective-permute-start.31
  357.6 27.6 %all-to-all-start.7 = ((bf16[8,192,256]{2,1,0:T(8,128)(2,1)}), bf16[8,192,256]{2,1,0:T(8,128)(2,1)}, u32[]{:S(2)}, u32[]{:S(2)}) async-start(bf16[8,192,256]{2,1,0:T(8,128)(2,1)} %added.11), calls=%async_computation.7 | async-start | bytes 1572864 | tf_op jit(solution)/shard_map/all_to_all | solution.py:1180
  373.6 8.4 %collective-permute-start.32 = (bf16[128,1024]{1,0:T(8,128)(2,1)}, bf16[128,1024]{1,0:T(8,128)(2,1)}, u32[]{:S(2)}, u32[]{:S(2)}) collective-permute-start(bf16[128,1024]{1,0:T(8,128)(2,1)} %slice.275), channel_id=1, source_target_pairs={{0,2},{1,3},{2,0},{3,1},{4,6},{5,7},{6,4},{7,5},{8,10},{9,11},{10,... | collective-permute-start | bytes 786440 | tf_op jit(solution)/shard_map/ppermute | solution.py:706
  390.5 3.8 collective-permute-start.33
  395.9 19.9 %collective-permute-start.34 = (bf16[256,1536]{1,0:T(8,128)(2,1)S(1)}, bf16[256,1536]{1,0:T(8,128)(2,1)S(1)}, u32[]{:S(2)}, u32[]{:S(2)}) collective-permute-start(bf16[256,1536]{1,0:T(8,128)(2,1)S(1)} %add_convert_fusion), channel_id=1, source_target_pairs={{0,4},{4,0},{8,12},{12,8},{16,20},{20,16},{24,28},{28,24},{1,5},{5... | collective-permute-start | bytes 2359304 | tf_op jit(solution)/shard_map/ppermute | solution.py:706
  398.3 6.0 %collective-permute-start.43 = (f32[8,128]{1,0:T(8,128)S(1)}, f32[8,128]{1,0:T(8,128)S(1)}, u32[]{:S(2)}, u32[]{:S(2)}) collective-permute-start(f32[8,128]{1,0:T(8,128)S(1)} %pad.9), channel_id=1, source_target_pairs={{0,1},{1,0},{2,3},{3,2},{4,5},{5,4},{6,7},{7,6},{8,9},{9,8},{10,11... | collective-permute-start | bytes 12296 | tf_op jit(solution)/shard_map/ppermute | solution.py:706
  399.8 16.0 %collective-permute-start.35 = (bf16[160,1024]{1,0:T(8,128)(2,1)S(1)}, bf16[160,1024]{1,0:T(8,128)(2,1)S(1)}, u32[]{:S(2)}, u32[]{:S(2)}) collective-permute-start(bf16[160,1024]{1,0:T(8,128)(2,1)S(1)} %get-tuple-element.252), channel_id=1, source_target_pairs={{0,8},{4,12},{8,0},{12,4},{16,24},{20,28},{24,16},{28,20},{1,9},{5... | collective-permute-start | bytes 983048 | tf_op jit(solution)/shard_map/ppermute | solution.py:706
  399.9 25.6 %collective-permute-start.41 = (bf16[160,1024]{1,0:T(8,128)(2,1)S(1)}, bf16[160,1024]{1,0:T(8,128)(2,1)S(1)}, u32[]{:S(2)}, u32[]{:S(2)}) collective-permute-start(bf16[160,1024]{1,0:T(8,128)(2,1)S(1)} %get-tuple-element.266), channel_id=1, source_target_pairs={{0,16},{4,20},{8,24},{12,28},{16,0},{20,4},{24,8},{28,12},{1,17},{... | collective-permute-start | bytes 983048 | tf_op jit(solution)/shard_map/ppermute | solution.py:706
  401.9 23.6 %collective-permute-start.42 = (bf16[160,1024]{1,0:T(8,128)(2,1)S(1)}, bf16[160,1024]{1,0:T(8,128)(2,1)S(1)}, u32[]{:S(2)}, u32[]{:S(2)}) collective-permute-start(bf16[160,1024]{1,0:T(8,128)(2,1)S(1)} %get-tuple-element.267), channel_id=1, source_target_pairs={{0,24},{4,28},{8,16},{12,20},{16,8},{20,12},{24,0},{28,4},{1,25},{... | collective-permute-start | bytes 983048 | tf_op jit(solution)/shard_map/ppermute | solution.py:706
  428.6 14.9 %collective-permute-start.37 = (bf16[64,1536]{1,0:T(8,128)(2,1)S(1)}, bf16[64,1536]{1,0:T(8,128)(2,1)S(1)}, u32[]{:S(2)}, u32[]{:S(2)}) collective-permute-start(bf16[64,1536]{1,0:T(8,128)(2,1)S(1)} %get-tuple-element.257), channel_id=1, source_target_pairs={{0,8},{4,12},{8,0},{12,4},{16,24},{20,28},{24,16},{28,20},{1,9},{5... | collective-permute-start | bytes 589832 | tf_op jit(solution)/shard_map/ppermute | solution.py:706
  435.9 17.2 %collective-permute-start.38 = (bf16[64,1536]{1,0:T(8,128)(2,1)S(1)}, bf16[64,1536]{1,0:T(8,128)(2,1)S(1)}, u32[]{:S(2)}, u32[]{:S(2)}) collective-permute-start(bf16[64,1536]{1,0:T(8,128)(2,1)S(1)} %get-tuple-element.258), channel_id=1, source_target_pairs={{0,16},{4,20},{8,24},{12,28},{16,0},{20,4},{24,8},{28,12},{1,17},{... | collective-permute-start | bytes 589832 | tf_op jit(solution)/shard_map/ppermute | solution.py:706
  435.9 17.1 %collective-permute-start.39 = (bf16[64,1536]{1,0:T(8,128)(2,1)S(1)}, bf16[64,1536]{1,0:T(8,128)(2,1)S(1)}, u32[]{:S(2)}, u32[]{:S(2)}) collective-permute-start(bf16[64,1536]{1,0:T(8,128)(2,1)S(1)} %get-tuple-element.259), channel_id=1, source_target_pairs={{0,24},{4,28},{8,16},{12,20},{16,8},{20,12},{24,0},{28,4},{1,25},{... | collective-permute-start | bytes 589832 | tf_op jit(solution)/shard_map/ppermute | solution.py:706
  438.3 16.4 %collective-permute-start.36 = (bf16[128,1024]{1,0:T(8,128)(2,1)S(1)}, bf16[128,1024]{1,0:T(8,128)(2,1)S(1)}, u32[]{:S(2)}, u32[]{:S(2)}) collective-permute-start(bf16[128,1024]{1,0:T(8,128)(2,1)S(1)} %slice.274), channel_id=1, source_target_pairs={{0,2},{1,3},{2,0},{3,1},{4,6},{5,7},{6,4},{7,5},{8,10},{9,11},{10,... | collective-permute-start | bytes 786440 | tf_op jit(solution)/shard_map/ppermute | solution.py:706
  439.8 18.3 %collective-permute-start.44 = (f32[32,2048]{1,0:T(8,128)S(1)}, f32[32,2048]{1,0:T(8,128)S(1)}, u32[]{:S(2)}, u32[]{:S(2)}) collective-permute-start(f32[32,2048]{1,0:T(8,128)S(1)} %broadcast_select_fusion.2), channel_id=1, source_target_pairs={{0,1},{1,0},{2,3},{3,2},{4,5},{5,4},{6,7},{7,6},{8,9},{9,8},{10,11... | collective-permute-start | bytes 786440 | tf_op jit(solution)/shard_map/ppermute | solution.py:706
  453.1 6.8 %collective-permute-start.40 = (f32[32,1536]{1,0:T(8,128)S(1)}, f32[32,1536]{1,0:T(8,128)S(1)}, u32[]{:S(2)}, u32[]{:S(2)}) collective-permute-start(f32[32,1536]{1,0:T(8,128)S(1)} %slice.230), channel_id=1, source_target_pairs={{0,2},{1,3},{2,0},{3,1},{4,6},{5,7},{6,4},{7,5},{8,10},{9,11},{10,... | collective-permute-start | bytes 589832 | tf_op jit(solution)/shard_map/ppermute | solution.py:706
  (76 other events, 554.6 us)
Sparse Core Ops, SparseCore 0:
  11.4 161.2 all-gather.2
